TPU v7x, 32 devices: a whole 2x2x4 slice. The times are simulated.
32 devices in a mesh: row: 4 (over y, core), col: 2 (over x), page: 4 (over z).
Axes of the slice: x: 2, y: 2, z: 4, core: 2. Of those that a mesh axis runs over, the one named last changes fastest.
Arguments:
- tokens: bfloat16 [16, 512, 2048], P(('row', 'page'), None, 'col'), may hold values from -6 to 6
- lengths: int32 [16], P(('row', 'page')), may hold values from 1 to 512, 2048 in all
- page_slot: int32 [16, 4], P('row'), may hold values from 0 to 15, as said below
- w_query: float32 [2048, 1024], P(('row', 'page'), 'col'), may hold values from -0.125 to 0.125
- w_keyval: float32 [2, 2048, 256], P(None, ('row', 'page')), may hold values from -0.125 to 0.125
- w_out: float32 [1024, 2048], P('col', ('row', 'page')), may hold values from -0.1875 to 0.1875
- w_gateup: float32 [2, 2048, 5120], P(None, ('row', 'page'), 'col'), may hold values from -0.125 to 0.125
- w_down: float32 [5120, 2048], P('col', ('row', 'page')), may hold values from -0.078125 to 0.078125
- attn_gain: float32 [2048], replicated, may hold values from 0.1 to 1.9
- ffn_gain: float32 [2048], replicated, may hold values from 0.1 to 1.9
- query_gain: float32 [64], replicated, may hold values from 0.1 to 1.9
- key_gain: float32 [64], replicated, may hold values from 0.1 to 1.9
Outputs:
- layer_out: bfloat16 [16, 512, 2048], P(('row', 'page'), None, 'col')
- kv_pages: bfloat16 [2, 64, 128, 1024], P(None, ('row', 'page'), None, 'col')
Inputs may be any that keep to these rules, and one draw needn't show every extreme that they name: `lengths`: each prompt's real tokens; in every draw some prompt has exactly 512. `page_slot`: within the prompts of one index of row the values are a permutation; page v belongs to index v // 4 of page; the 4 blocks of the prompts of one device send the same number of blocks to each of the 4 indices of page.
All inputs are finite; a program needn't handle non-finite values. No bound on the sum of `lengths` on one device may be relied on, other than what follows from the above.
Results may differ from a plain program's by a relative error of at most 0.012.
Values may be sent and summed in bfloat16 or wider, within the bound.
A program may use at most 128 MiB of HBM per device.

v0:
```python
import jax
import jax.numpy as jnp
from jax import lax
from jax.sharding import PartitionSpec as P

PAGE_LEN = 128


def normalize(values, norm_gain):
    mean_sq = jnp.mean(values * values, axis=-1, keepdims=True)
    return values * lax.rsqrt(mean_sq + 1e-06) * norm_gain


def rotate(values):
    row_count = values.shape[-3]
    head_dim = values.shape[-1]
    half_dim = head_dim // 2
    frequency = 10000.0 ** (-2.0 * jnp.arange(half_dim, dtype=jnp.float32) / head_dim)
    angles = jnp.arange(row_count, dtype=jnp.float32)[:, None] * frequency[None, :]
    cosine = jnp.cos(angles)[:, None, :]
    sine_table = jnp.sin(angles)[:, None, :]
    leading = values[..., :half_dim]
    trailing = values[..., half_dim:]
    return jnp.concatenate(
        [leading * cosine - trailing * sine_table, trailing * cosine + leading * sine_table],
        axis=-1,
    )


def attend(query_rows, key_rows, value_rows, length):
    row_count = query_rows.shape[0]
    scores = jnp.einsum(
        "qhd,khd->hqk", query_rows, key_rows, preferred_element_type=jnp.float32
    ) * query_rows.shape[2] ** (-0.5)
    positions = jnp.arange(row_count, dtype=jnp.int32)
    seen_keys = (positions[None, :] <= positions[:, None]) & (positions[None, :] < length)
    exp_scores = jnp.where(seen_keys[None], jnp.exp(scores), 0.0)
    attn_probs = (exp_scores / jnp.sum(exp_scores, axis=-1, keepdims=True)).astype(jnp.bfloat16)
    attended = jnp.einsum(
        "hqk,khd->qhd", attn_probs, value_rows, preferred_element_type=jnp.float32
    )
    live_rows = (positions < length)[:, None, None]
    return jnp.where(live_rows, attended, 0.0).astype(jnp.bfloat16)


def on_device(
    tokens,
    lengths,
    page_slot,
    w_query,
    w_keyval,
    w_out,
    w_gateup,
    w_down,
    attn_gain,
    ffn_gain,
    query_gain,
    key_gain,
):
    col_count = lax.axis_size("col")
    col_index = lax.axis_index("col")
    head_dim = query_gain.shape[0]
    local_width = w_query.shape[1]
    local_heads = local_width // head_dim
    kv_heads = w_keyval.shape[2] // head_dim
    group_size = local_heads * col_count // kv_heads
    kv_index = (col_index * local_heads + jnp.arange(local_heads, dtype=jnp.int32)) // group_size
    columns = (
        kv_index[:, None] * head_dim + jnp.arange(head_dim, dtype=jnp.int32)[None, :]
    ).reshape(-1)
    keyval_piece = w_keyval.astype(jnp.bfloat16)
    query_piece = w_query.astype(jnp.bfloat16)
    out_piece = w_out.astype(jnp.bfloat16)
    gateup_piece = w_gateup.astype(jnp.bfloat16)
    down_piece = w_down.astype(jnp.bfloat16)
    query_full, keyval_full, out_full, gateup_full, down_full = (
        lax.all_gather(query_piece, ("row", "page"), axis=0, tiled=True),
        lax.all_gather(keyval_piece, ("row", "page"), axis=1, tiled=True),
        lax.all_gather(out_piece, ("row", "page"), axis=1, tiled=True),
        lax.all_gather(gateup_piece, ("row", "page"), axis=1, tiled=True),
        lax.all_gather(down_piece, ("row", "page"), axis=1, tiled=True),
    )
    keyval_used = jnp.take(keyval_full, columns, axis=2)
    merged_qkv = jnp.concatenate([query_full, keyval_used[0], keyval_used[1]], axis=1)
    merged_gateup = jnp.concatenate([gateup_full[0], gateup_full[1]], axis=1)
    prompt_count, seq_len, local_feat = tokens.shape
    gathered = lax.all_gather(tokens, "col", axis=2, tiled=True)
    model_width = gathered.shape[2]
    attn_in = normalize(gathered.astype(jnp.float32), attn_gain).astype(jnp.bfloat16)
    projected = jnp.dot(
        attn_in.reshape(-1, model_width), merged_qkv, preferred_element_type=jnp.float32
    )
    projected = projected.reshape(prompt_count, seq_len, 3, local_heads, head_dim)
    queries = rotate(normalize(projected[:, :, 0], query_gain)).astype(jnp.bfloat16)
    keys_rot = rotate(normalize(projected[:, :, 1], key_gain)).astype(jnp.bfloat16)
    values_in = projected[:, :, 2].astype(jnp.bfloat16)
    attended_one = attend(queries[0], keys_rot[0], values_in[0], lengths[0])
    outputs = [attended_one.reshape(seq_len, local_width)]
    attended = jnp.stack(outputs)
    attn_terms = jnp.dot(
        attended.reshape(-1, local_width), out_full, preferred_element_type=jnp.float32
    )
    attn_terms = attn_terms.reshape(prompt_count, seq_len, model_width)
    attn_sum = lax.psum_scatter(
        attn_terms.astype(jnp.bfloat16), "col", scatter_dimension=2, tiled=True
    ).astype(jnp.float32)
    residual = (tokens.astype(jnp.float32) + attn_sum).astype(jnp.bfloat16)
    residual_all = lax.all_gather(residual, "col", axis=2, tiled=True)
    ffn_in = normalize(residual_all.astype(jnp.float32), ffn_gain).astype(jnp.bfloat16)
    gate_up = jnp.dot(
        ffn_in.reshape(-1, model_width), merged_gateup, preferred_element_type=jnp.float32
    )
    unit_count = gateup_full.shape[2]
    hidden = (jax.nn.silu(gate_up[:, :unit_count]) * gate_up[:, unit_count:]).astype(jnp.bfloat16)
    ffn_terms = jnp.dot(hidden, down_full, preferred_element_type=jnp.float32).reshape(
        prompt_count, seq_len, model_width
    )
    ffn_sum = lax.psum_scatter(
        ffn_terms.astype(jnp.bfloat16), "col", scatter_dimension=2, tiled=True
    ).astype(jnp.float32)
    layer_out = (residual.astype(jnp.float32) + ffn_sum).astype(jnp.bfloat16)
    page_count = lax.axis_size("page")
    page_index = lax.axis_index("page")
    blocks_each = prompt_count * (seq_len // PAGE_LEN)
    capacity = blocks_each // page_count
    owners = page_slot // blocks_each
    local_slot = page_slot % blocks_each
    same_owner = owners[:, :, None] == owners[:, None, :]
    earlier = (
        jnp.arange(blocks_each, dtype=jnp.int32)[None, :]
        < jnp.arange(blocks_each, dtype=jnp.int32)[:, None]
    )
    order_in = jnp.sum((same_owner & earlier[None]).astype(jnp.int32), axis=2)
    my_owners = lax.dynamic_index_in_dim(owners, page_index, 0, keepdims=False)
    my_order = lax.dynamic_index_in_dim(order_in, page_index, 0, keepdims=False)
    send_pos = my_owners * capacity + my_order
    live_rows = (jnp.arange(seq_len, dtype=jnp.int32)[None, :] < lengths[:, None])[:, :, None, None]
    page_keys = jnp.where(live_rows, keys_rot, jnp.zeros_like(keys_rot)).reshape(
        blocks_each, PAGE_LEN, local_width
    )
    page_values = jnp.where(live_rows, values_in, jnp.zeros_like(values_in)).reshape(
        blocks_each, PAGE_LEN, local_width
    )
    stacked = jnp.stack([page_keys, page_values])
    outgoing = jnp.zeros_like(stacked).at[:, send_pos].set(stacked)
    incoming = lax.all_to_all(outgoing, "page", split_axis=1, concat_axis=1, tiled=True)
    arrival_hit = (owners[:, None, :] == page_index) & (
        order_in[:, None, :] == jnp.arange(capacity, dtype=jnp.int32)[None, :, None]
    )
    arrival_slot = jnp.sum(jnp.where(arrival_hit, local_slot[:, None, :], 0), axis=2).reshape(
        blocks_each
    )
    kv_pages = jnp.zeros_like(incoming).at[:, arrival_slot].set(incoming)
    return (layer_out, kv_pages)


def solution(mesh):
    in_specs = (
        P(("row", "page"), None, "col"),
        P(("row", "page")),
        P("row", None),
        P(("row", "page"), "col"),
        P(None, ("row", "page"), None),
        P("col", ("row", "page")),
        P(None, ("row", "page"), "col"),
        P("col", ("row", "page")),
        P(),
        P(),
        P(),
        P(),
    )
    out_specs = (P(("row", "page"), None, "col"), P(None, ("row", "page"), None, "col"))
    return jax.shard_map(
        on_device, mesh=mesh, in_specs=in_specs, out_specs=out_specs, check_vma=False
    )
```

profile of v0, /device:TPU:17, one launch (start us, length us, event | category | flops | bytes accessed | tf_op | source)
XLA Modules:
  0.0 517.5 jit_solution(12587585154824484044)
XLA Ops:
  7.2 0.7 all-gather.8.cloned.1.call-update
  7.9 1.8 copy.50
  9.8 1.6 convert_element_type.114
  11.5 1.6 convert_element_type.121
  13.5 0.3 fusion.43
  14.5 0.8 fusion.31
  15.3 28.5 %all-gather.8.cloned.1.call-done = bf16[1,512,2048]{2,1,0:T(8,128)(2,1)} async-done(((bf16[1,512,1024]{2,1,0:T(8,128)(2,1)}), bf16[1,512,2048]{2,1,0:T(8,128)(2,1)}) %all-gather.8.cloned.1.call-update) | async-done | bytes 2097168 | tf_op jit(solution)/shard_map/all_gather | solution.py:87
  43.8 2.1 fusion.6
  45.8 48.5 %all-gather.12.cloned.1.call-done = bf16[2,2048,256]{1,0,2:T(2,128)(2,1)} async-done(((bf16[2,128,256]{1,0,2:T(2,128)(2,1)}), bf16[2,2048,256]{1,0,2:T(2,128)(2,1)}) %all-gather.12.cloned.1.call-update) | async-done | bytes 2097168 | tf_op jit(solution)/shard_map/all_gather | solution.py:78
  94.3 19.9 %gather_fusion = bf16[512,2,2048]{2,1,0:T(2,128)(2,1)} fusion(bf16[2,2048,256]{1,0,2:T(2,128)(2,1)} %all-gather.12.cloned.1.call-done, s32[1024]{0:T(1024)S(1)} %pad_clamp_fusion), kind=kCustom, calls=%fused_computation | custom fusion | bytes 8390656 | tf_op jit(solution)/shard_map/jit(_take)/gather | solution.py:83
  114.2 8.2 %fusion.12 = bf16[2,2048,512]{1,0,2:T(2,128)(2,1)} fusion(bf16[512,2,2048]{2,1,0:T(2,128)(2,1)} %gather_fusion, pred[512]{0:T(512)(128)(4,1)S(1)} %compare_and_fusion), kind=kLoop, calls=%fused_computation.26 | loop fusion | flops 2097152 | bytes 8389120 | tf_op jit(solution)/shard_map/jit(_take)/select_n | solution.py:83
  122.4 10.2 %fusion.55 = (bf16[1,2048,512]{1,0,2:T(2,128)(2,1)}, bf16[1,2048,512]{1,0,2:T(2,128)(2,1)}) fusion(bf16[2,2048,512]{1,0,2:T(2,128)(2,1)} %fusion.12), kind=kLoop, calls=%fused_computation.112 | loop fusion | bytes 8388608 | tf_op jit(solution)/shard_map/slice | solution.py:84
  132.5 9.0 %copy.51 = bf16[1,2048,512]{2,1,0:T(8,128)(2,1)S(1)} copy(bf16[1,2048,512]{1,0,2:T(2,128)(2,1)} %get-tuple-element.6) | data formatting | bytes 4194304 | tf_op jit(solution)/shard_map/slice | solution.py:84
  141.5 10.5 %copy.52 = bf16[1,2048,512]{2,1,0:T(8,128)(2,1)} copy(bf16[1,2048,512]{1,0,2:T(2,128)(2,1)} %get-tuple-element.7) | data formatting | bytes 4194304 | tf_op jit(solution)/shard_map/slice | solution.py:84
  152.0 5.4 %maximum_bitcast_fusion = bf16[1536,2048]{0,1:T(8,128)(2,1)} fusion(bf16[2048,512]{1,0:T(8,128)(2,1)} %bitcast.81, bf16[2048,512]{1,0:T(8,128)(2,1)S(1)} %bitcast.80, bf16[2048,512]{1,0:T(8,128)(2,1)} %all-gather.10.cloned.1.call-done), kind=kLoop, calls=%fused_computation.13 | loop fusion | flops 18874368 | bytes 12582912 | tf_op jit(solution)/shard_map/dot_general | solution.py:90
  157.4 8.7 %copy.53 = bf16[1536,2048]{1,0:T(8,128)(2,1)} copy(bf16[1536,2048]{0,1:T(8,128)(2,1)} %maximum_bitcast_fusion) | data formatting | bytes 12582912 | tf_op jit(solution)/shard_map/dot_general | solution.py:90
  166.1 6.6 %fusion.26 = f32[1,512,3,8,64]{1,4,3,2,0:T(8,128)S(1)} fusion(bf16[3,8,64,2048]{3,2,1,0:T(8,128)(2,1)} %bitcast.82, bf16[1,512,2048]{2,1,0:T(8,128)(2,1)} %all-gather.8.cloned.1.call-done, f32[2048]{0:T(1024)S(1)} %copy-done.8, f32[512]{0:T(512)S(1)} %add_rsqrt_fusion.3), kind=kOutput, calls=%fused_computation.41 | convolution fusion | flops 3225419776 | bytes 11544576 | tf_op jit(solution)/shard_map/dot_general | solution.py:90
  172.7 0.3 multiply_reduce_fusion
  173.1 0.5 multiply_multiply_fusion
  173.5 0.4 subtract_convert_fusion
  174.0 2.2 fusion.4
  176.2 2.9 fusion.30
  179.1 4.4 fusion.15
  183.6 31.6 %reduce-scatter.3.cloned.1.call-done = bf16[1,512,1024]{2,1,0:T(8,128)(2,1)} async-done(((bf16[1,512,2048]{2,1,0:T(8,128)(2,1)}), bf16[1,512,1024]{2,1,0:T(8,128)(2,1)}) %reduce-scatter.3.cloned.1.call-update) | async-done | bytes 1048592 | tf_op jit(solution)/shard_map/reduce_scatter | solution.py:104
  215.1 2.9 add_convert_fusion.1
  218.1 3.0 convert_element_type.129
  221.1 2.2 convert_element_type.131
  223.4 27.9 %all-gather.16.cloned.1.call-done = bf16[1,512,2048]{2,1,0:T(8,128)(2,1)} async-done(((bf16[1,512,1024]{2,1,0:T(8,128)(2,1)}), bf16[1,512,2048]{2,1,0:T(8,128)(2,1)}) %all-gather.16.cloned.1.call-update) | async-done | bytes 2097168 | tf_op jit(solution)/shard_map/all_gather | solution.py:108
  251.3 2.1 fusion.9
  253.4 114.0 %all-gather.18.cloned.1.call-done = bf16[2,2048,2560]{2,1,0:T(8,128)(2,1)} async-done(((bf16[2,128,2560]{2,1,0:T(8,128)(2,1)}), bf16[2,2048,2560]{2,1,0:T(8,128)(2,1)}) %all-gather.18.cloned.1.call-update) | async-done | bytes 20971536 | tf_op jit(solution)/shard_map/all_gather | solution.py:80
  367.5 16.1 %slice_bitcast_fusion.1 = (bf16[2048,2560]{1,0:T(8,128)(2,1)}, bf16[2048,2560]{1,0:T(8,128)(2,1)}) fusion(bf16[2,2048,2560]{2,1,0:T(8,128)(2,1)} %all-gather.18.cloned.1.call-done), kind=kLoop, calls=%fused_computation.8 | loop fusion | bytes 41943040 | tf_op jit(solution)/shard_map/squeeze | solution.py:85
  383.5 17.9 %fusion = f32[512,5120]{1,0:T(8,128)} fusion(bf16[2048,2560]{1,0:T(8,128)(2,1)} %get-tuple-element.5, bf16[2048,2560]{1,0:T(8,128)(2,1)} %get-tuple-element.4, bf16[1,512,2048]{2,1,0:T(8,128)(2,1)S(1)} %copy-done.2, f32[2048]{0:T(1024)S(1)} %copy-done.9, f32[512]{0:T(512)S(1)} %add_rsqrt_fusion.2), kind=kOutput, calls=%fused_computation.3 | convolution fusion | flops 10783555584 | bytes 33564672 | tf_op jit(solution)/shard_map/dot_general | solution.py:110
  401.4 59.5 %all-gather.20.cloned.1.call-done = bf16[2560,2048]{1,0:T(8,128)(2,1)} async-done(((bf16[2560,128]{1,0:T(8,128)(2,1)}), bf16[2560,2048]{1,0:T(8,128)(2,1)}) %all-gather.20.cloned.1.call-update) | async-done | bytes 10485776 | tf_op jit(solution)/shard_map/all_gather | solution.py:81
  460.9 12.5 %fusion.14 = bf16[1,512,2048]{2,1,0:T(8,128)(2,1)} fusion(bf16[2560,2048]{1,0:T(8,128)(2,1)} %all-gather.20.cloned.1.call-done, f32[512,5120]{1,0:T(8,128)} %fusion), kind=kOutput, calls=%fused_computation.30 | convolution fusion | flops 5377622016 | bytes 23068672 | tf_op jit(solution)/shard_map/dot_general | solution.py:115
  473.4 0.2 convert_reduce_fusion
  473.7 0.9 slice.102
  474.5 1.0 pad_maximum_fusion
  475.5 0.1 convert_element_type.137
  475.7 0.3 copy.55
  476.0 1.2 convert_element_type.138
  477.2 0.3 copy.56
  477.5 0.1 broadcast_select_fusion.2
  477.8 0.8 scatter_fusion
  478.7 1.1 copy.57
  479.8 4.6 all-to-all-start
  484.5 22.5 %all-to-all-done = bf16[2,4,128,512]{3,2,0,1:T(8,128)(2,1)S(1)} async-done(((bf16[2,4,128,512]{3,2,0,1:T(8,128)(2,1)}), bf16[2,4,128,512]{3,2,0,1:T(8,128)(2,1)S(1)}, u32[]{:S(2)}, u32[]{:S(2)}) %all-to-all-start) | async-done | bytes 1048608 | tf_op jit(solution)/shard_map/all_to_all | solution.py:146
  507.1 0.8 scatter_fusion.1
  508.0 2.9 add_convert_fusion
  (61 shorter events, 1.4 us)
Async XLA Ops:
  7.2 36.6 %all-gather.8.cloned.1.call-start = ((), (), s32[]{:S(2)}) async-start(), calls=%async_computation.3 | async-start | bytes 3145728 | tf_op jit(solution)/shard_map/all_gather | solution.py:87
  7.9 86.4 %all-gather.12.cloned.1.call-start = ((), (), s32[]{:S(2)}) async-start(), calls=%async_computation.5 | async-start | bytes 2228224 | tf_op jit(solution)/shard_map/all_gather | solution.py:78
  9.7 142.3 %all-gather.10.cloned.1.call-start = ((), (), s32[]{:S(2)}) async-start(), calls=%async_computation.4 | async-start | bytes 2228224 | tf_op jit(solution)/shard_map/all_gather | solution.py:77
  11.4 167.7 %all-gather.14.cloned.1.call-start = ((), (), s32[]{:S(2)}) async-start(), calls=%async_computation.6 | async-start | bytes 2228224 | tf_op jit(solution)/shard_map/all_gather | solution.py:79
  13.1 202.0 %reduce-scatter.3.cloned.1.call-start = ((), (), s32[]{:S(2)}) async-start(), calls=%async_computation.7 | async-start | bytes 3145728 | tf_op jit(solution)/shard_map/reduce_scatter | solution.py:104
  157.4 8.7 %copy-start.8 = (f32[2048]{0:T(1024)S(1)}, f32[2048]{0:T(1024)}, u32[]{:S(2)}) copy-start(f32[2048]{0:T(1024)} %param.20) | copy-start | bytes 24580
  166.1 7.0 %copy-start.6 = (f32[64]{0:T(128)S(1)}, f32[64]{0:T(128)}, u32[]{:S(2)}) copy-start(f32[64]{0:T(128)} %param.23) | copy-start | bytes 772
  166.1 7.0 %copy-start.7 = (f32[64]{0:T(128)S(1)}, f32[64]{0:T(128)}, u32[]{:S(2)}) copy-start(f32[64]{0:T(128)} %param.22) | copy-start | bytes 772
  173.0 1.0 copy-start.4
  173.9 2.3 copy-start.3
  183.5 67.8 %all-gather.16.cloned.1.call-start = ((), (), s32[]{:S(2)}) async-start(), calls=%async_computation.8 | async-start | bytes 3145728 | tf_op jit(solution)/shard_map/all_gather | solution.py:108
  218.1 149.4 %all-gather.18.cloned.1.call-start = ((), (), s32[]{:S(2)}) async-start(), calls=%async_computation.9 | async-start | bytes 22282240 | tf_op jit(solution)/shard_map/all_gather | solution.py:80
  221.1 239.8 %all-gather.20.cloned.1.call-start = ((), (), s32[]{:S(2)}) async-start(), calls=%async_computation.10 | async-start | bytes 11141120 | tf_op jit(solution)/shard_map/all_gather | solution.py:81
  223.4 284.6 %reduce-scatter.5.cloned.1.call-start = ((), (), s32[]{:S(2)}) async-start(), calls=%async_computation.11 | async-start | bytes 3145728 | tf_op jit(solution)/shard_map/reduce_scatter | solution.py:118
  253.4 130.1 %copy-start.9 = (f32[2048]{0:T(1024)S(1)}, f32[2048]{0:T(1024)}, u32[]{:S(2)}) copy-start(f32[2048]{0:T(1024)} %param.21) | copy-start | bytes 24580
  367.4 16.1 %copy-start.2 = (bf16[1,512,2048]{2,1,0:T(8,128)(2,1)S(1)}, bf16[1,512,2048]{2,1,0:T(8,128)(2,1)}, u32[]{:S(2)}) copy-start(bf16[1,512,2048]{2,1,0:T(8,128)(2,1)} %all-gather.16.cloned.1.call-done) | copy-start | bytes 6291460
  401.4 72.0 %copy-start.5 = (s32[4,4]{1,0:T(4,128)S(1)}, s32[4,4]{1,0:T(4,128)}, u32[]{:S(2)}) copy-start(s32[4,4]{1,0:T(4,128)} %param.14) | copy-start | bytes 196
  478.7 29.3 %copy-start = (bf16[1,512,1024]{2,1,0:T(8,128)(2,1)S(1)}, bf16[1,512,1024]{2,1,0:T(8,128)(2,1)}, u32[]{:S(2)}) copy-start(bf16[1,512,1024]{2,1,0:T(8,128)(2,1)} %add_convert_fusion.1) | copy-start | bytes 3145732
  479.8 27.3 %all-to-all-start = ((bf16[2,4,128,512]{3,2,0,1:T(8,128)(2,1)}), bf16[2,4,128,512]{3,2,0,1:T(8,128)(2,1)S(1)}, u32[]{:S(2)}, u32[]{:S(2)}) async-start(bf16[2,4,128,512]{3,2,0,1:T(8,128)(2,1)} %copy.57), calls=%async_computation.2 | async-start | bytes 2097152 | tf_op jit(solution)/shard_map/all_to_all | solution.py:146
  508.0 3.0 copy-start.1
Sparse Core Ops, SparseCore 0:
  9.5 34.1 all-gather.7
  46.4 47.9 all-gather.11
  96.6 39.6 all-gather.9
  138.2 40.6 all-gather.13
  183.6 31.4 reduce-scatter.2
  218.2 33.0 all-gather.15
  253.0 114.4 all-gather.17
  370.3 90.5 all-gather.19
  473.5 30.4 reduce-scatter.4
where the time goes:
time: 524 us; the launch traced here: 517 us
  waiting for transfers between devices  333 us (64%)
  local copies, waits for them, and re-layouts  82 us (16%)
  matrix products  46.5 us (9%)
  other arithmetic  36 us (7%)
  between operations  14.8 us (3%)
    all_gather x1, waiting for transfers between devices, on_device(): lax.all_gather(gateup_piece, ('row', 'page'), axis=1, tiled=True)  114 us
    all_gather x1, waiting for transfers between devices, on_device(): lax.all_gather(down_piece, ('row', 'page'), axis=1, tiled=True)  59.5 us
    all_gather x1, waiting for transfers between devices, on_device(): lax.all_gather(keyval_piece, ('row', 'page'), axis=1, tiled=True)  48.5 us
    reduce_scatter x1, waiting for transfers between devices, on_device(): lax.psum_scatter(attn_terms.astype(jnp.bfloat16), 'col', scatter_dimensio...  31.6 us
    all_gather x1, waiting for transfers between devices, on_device(): gathered = lax.all_gather(tokens, 'col', axis=2, tiled=True)  28.5 us
    all_gather x1, waiting for transfers between devices, on_device(): residual_all = lax.all_gather(residual, 'col', axis=2, tiled=True)  27.9 us
    all_to_all x1, waiting for transfers between devices, on_device(): lax.all_to_all(outgoing, 'page', split_axis=1, concat_axis=1, tiled=True)  22.5 us
    gather x1, local copies, waits for them, and re-layouts, on_device(): keyval_used = jnp.take(keyval_full, columns, axis=2)  19.9 us
  transfers between devices with their start and end apart: 10, of which 7 were waited for; matrix products, arithmetic and copies ran while one was open for 27% of the time, Pallas kernels for 0%

commit v1 on v0

v1 whole, which is shorter than its diff:
```python
import jax
import jax.numpy as jnp
from jax import lax
from jax.experimental.layout import Layout, with_layout_constraint
from jax.sharding import PartitionSpec as P

PAGE_LEN = 128


def normalize(values, norm_gain):
    mean_sq = jnp.mean(values * values, axis=-1, keepdims=True)
    return values * lax.rsqrt(mean_sq + 1e-06) * norm_gain


def rotate(values):
    row_count = values.shape[-3]
    head_dim = values.shape[-1]
    half_dim = head_dim // 2
    frequency = 10000.0 ** (-2.0 * jnp.arange(half_dim, dtype=jnp.float32) / head_dim)
    angles = jnp.arange(row_count, dtype=jnp.float32)[:, None] * frequency[None, :]
    cosine = jnp.cos(angles)[:, None, :]
    sine_table = jnp.sin(angles)[:, None, :]
    leading = values[..., :half_dim]
    trailing = values[..., half_dim:]
    return jnp.concatenate(
        [leading * cosine - trailing * sine_table, trailing * cosine + leading * sine_table],
        axis=-1,
    )


def attend(query_rows, key_rows, value_rows, length):
    kv_count, row_count, group, head_dim = query_rows.shape
    scores = jnp.einsum(
        "gqre,gke->grqk", query_rows, key_rows, preferred_element_type=jnp.float32
    ) * head_dim ** (-0.5)
    positions = jnp.arange(row_count, dtype=jnp.int32)
    seen_keys = (positions[None, :] <= positions[:, None]) & (positions[None, :] < length)
    exp_scores = jnp.where(seen_keys, jnp.exp(scores), 0.0)
    attn_probs = (exp_scores / jnp.sum(exp_scores, axis=-1, keepdims=True)).astype(jnp.bfloat16)
    attended = jnp.einsum(
        "grqk,gke->qgre", attn_probs, value_rows, preferred_element_type=jnp.float32
    )
    live_rows = (positions < length)[:, None, None, None]
    return jnp.where(live_rows, attended, 0.0).astype(jnp.bfloat16)


def gather_col(values, col_count, col_index):
    if col_count != 2:
        return lax.all_gather(values, "col", axis=values.ndim - 1, tiled=True)
    other = lax.ppermute(values, "col", [(0, 1), (1, 0)])
    first = jnp.where(col_index == 0, values, other)
    second = jnp.where(col_index == 0, other, values)
    return jnp.concatenate([first, second], axis=-1)


def gather_rows(piece):
    rows_major = Layout(major_to_minor=(0, 1))
    piece = with_layout_constraint(piece, rows_major)
    full = lax.all_gather(piece, ("row", "page"), axis=0, tiled=True)
    return with_layout_constraint(full, rows_major)


def on_device(
    tokens,
    lengths,
    page_slot,
    w_query,
    w_keyval,
    w_out,
    w_gateup,
    w_down,
    attn_gain,
    ffn_gain,
    query_gain,
    key_gain,
):
    bf16 = jnp.bfloat16
    f32 = jnp.float32
    col_count = lax.axis_size("col")
    col_index = lax.axis_index("col")
    head_dim = query_gain.shape[0]
    local_width = w_query.shape[1]
    local_heads = local_width // head_dim
    kv_heads = w_keyval.shape[2] // head_dim
    group_size = local_heads * col_count // kv_heads
    kv_count = max(1, local_heads // group_size)
    rep = local_heads // kv_count
    kv_width = kv_count * head_dim
    kv_start = (col_index * local_heads // group_size) * head_dim
    prompt_count, seq_len, local_feat = tokens.shape
    model_width = attn_gain.shape[0]
    unit_count = w_gateup.shape[2]

    gathered = gather_col(tokens, col_count, col_index)

    keyval_piece = lax.dynamic_slice_in_dim(w_keyval, kv_start, kv_width, axis=2)
    attn_piece = jnp.concatenate(
        [w_query, keyval_piece[0], keyval_piece[1], w_out.T], axis=1
    ).astype(bf16)
    gateup_piece = jnp.concatenate([w_gateup[0], w_gateup[1]], axis=1).astype(bf16)
    down_piece = w_down.T.astype(bf16)
    attn_full = gather_rows(attn_piece)
    gateup_full = gather_rows(gateup_piece)
    down_full = gather_rows(down_piece)
    qkv_width = local_width + 2 * kv_width
    out_t = attn_full[:, qkv_width:]

    attn_in = normalize(gathered.astype(f32), attn_gain).astype(bf16)
    projected = jnp.dot(
        attn_in.reshape(-1, model_width), attn_full[:, :qkv_width], preferred_element_type=f32
    ).reshape(prompt_count, seq_len, qkv_width)
    heads = projected[:, :, : local_width + kv_width].reshape(
        prompt_count, seq_len, local_heads + kv_count, head_dim
    )
    gains = jnp.concatenate(
        [
            jnp.broadcast_to(query_gain, (local_heads, head_dim)),
            jnp.broadcast_to(key_gain, (kv_count, head_dim)),
        ]
    )
    rotated = rotate(normalize(heads, gains)).astype(bf16)
    values_in = projected[:, :, local_width + kv_width :].astype(bf16)
    keys_rot = rotated[:, :, local_heads:]
    parts = []
    for prompt in range(prompt_count):
        query_rows = rotated[prompt, :, :local_heads].reshape(seq_len, kv_count, rep, head_dim)
        parts.append(
            attend(
                query_rows.transpose(1, 0, 2, 3),
                keys_rot[prompt].transpose(1, 0, 2),
                values_in[prompt].reshape(seq_len, kv_count, head_dim).transpose(1, 0, 2),
                lengths[prompt],
            ).reshape(seq_len, local_width)
        )
    attended = jnp.stack(parts).reshape(-1, local_width)
    attn_terms = lax.dot_general(
        attended, out_t, (((1,), (1,)), ((), ())), preferred_element_type=f32
    ).astype(bf16).reshape(prompt_count, seq_len, model_width)

    if col_count == 2:
        attn_other = lax.ppermute(attn_terms, "col", [(0, 1), (1, 0)])
        attn_sum = attn_terms.astype(f32) + attn_other.astype(f32)
        residual_all = (gathered.astype(f32) + attn_sum).astype(bf16)
        residual = lax.dynamic_slice_in_dim(
            residual_all, col_index * local_feat, local_feat, axis=2
        )
    else:
        attn_sum = lax.psum_scatter(attn_terms, "col", scatter_dimension=2, tiled=True)
        residual = (tokens.astype(f32) + attn_sum.astype(f32)).astype(bf16)
        residual_all = lax.all_gather(residual, "col", axis=2, tiled=True)

    page_count = lax.axis_size("page")
    page_index = lax.axis_index("page")
    blocks_each = prompt_count * (seq_len // PAGE_LEN)
    capacity = blocks_each // page_count
    owners = page_slot // blocks_each
    local_slot = page_slot % blocks_each
    owners = owners.reshape(page_count, blocks_each)
    local_slot = local_slot.reshape(page_count, blocks_each)
    same_owner = owners[:, :, None] == owners[:, None, :]
    earlier = (
        jnp.arange(blocks_each, dtype=jnp.int32)[None, :]
        < jnp.arange(blocks_each, dtype=jnp.int32)[:, None]
    )
    order_in = jnp.sum((same_owner & earlier[None]).astype(jnp.int32), axis=2)
    my_owners = lax.dynamic_index_in_dim(owners, page_index, 0, keepdims=False)
    my_order = lax.dynamic_index_in_dim(order_in, page_index, 0, keepdims=False)
    send_pos = my_owners * capacity + my_order
    live_rows = (jnp.arange(seq_len, dtype=jnp.int32)[None, :] < lengths[:, None])[:, :, None]
    keys_flat = keys_rot.reshape(prompt_count, seq_len, kv_width)
    both = jnp.stack([keys_flat, values_in])
    both = jnp.where(live_rows[None], both, jnp.zeros_like(both)).reshape(
        2, blocks_each, PAGE_LEN, kv_width
    )
    from_block = jnp.argmax(
        send_pos[None, :] == jnp.arange(blocks_each, dtype=jnp.int32)[:, None], axis=1
    )
    outgoing = jnp.take(both, from_block, axis=1)
    incoming = lax.all_to_all(outgoing, "page", split_axis=1, concat_axis=1, tiled=True)
    arrival_hit = (owners[:, None, :] == page_index) & (
        order_in[:, None, :] == jnp.arange(capacity, dtype=jnp.int32)[None, :, None]
    )
    arrival_slot = jnp.sum(jnp.where(arrival_hit, local_slot[:, None, :], 0), axis=2).reshape(
        blocks_each
    )
    from_arrival = jnp.argmax(
        arrival_slot[None, :] == jnp.arange(blocks_each, dtype=jnp.int32)[:, None], axis=1
    )
    placed = jnp.take(incoming, from_arrival, axis=1)
    kv_pages = jnp.concatenate(
        [
            placed[..., head * head_dim : (head + 1) * head_dim]
            for head in range(kv_count)
            for _ in range(rep)
        ],
        axis=-1,
    )

    ffn_in = normalize(residual_all.astype(f32), ffn_gain).astype(bf16)
    gate_up = jnp.dot(
        ffn_in.reshape(-1, model_width), gateup_full, preferred_element_type=f32
    )
    hidden = (jax.nn.silu(gate_up[:, :unit_count]) * gate_up[:, unit_count:]).astype(bf16)
    kv_pages, hidden = lax.optimization_barrier((kv_pages, hidden))
    contract_last = (((1,), (1,)), ((), ()))
    if col_count == 2:
        other_w = lax.dynamic_slice_in_dim(down_full, (1 - col_index) * local_feat, local_feat, 0)
        own_w = lax.dynamic_slice_in_dim(down_full, col_index * local_feat, local_feat, 0)
        theirs = lax.dot_general(
            hidden, other_w, contract_last, preferred_element_type=f32
        ).astype(bf16)
        arrived = lax.ppermute(theirs, "col", [(0, 1), (1, 0)])
        mine = lax.dot_general(
            hidden, own_w, contract_last, preferred_element_type=f32
        ).astype(bf16)
        mine = lax.optimization_barrier(mine)
        ffn_sum = (mine.astype(f32) + arrived.astype(f32)).reshape(
            prompt_count, seq_len, local_feat
        )
    else:
        ffn_terms = lax.dot_general(
            hidden, down_full, contract_last, preferred_element_type=f32
        ).astype(bf16)
        ffn_sum = lax.psum_scatter(
            ffn_terms.reshape(prompt_count, seq_len, model_width),
            "col",
            scatter_dimension=2,
            tiled=True,
        ).astype(f32)
    layer_out = (residual.astype(f32) + ffn_sum).astype(bf16)
    return (layer_out, kv_pages)


def solution(mesh):
    in_specs = (
        P(("row", "page"), None, "col"),
        P(("row", "page")),
        P("row", None),
        P(("row", "page"), "col"),
        P(None, ("row", "page"), None),
        P("col", ("row", "page")),
        P(None, ("row", "page"), "col"),
        P("col", ("row", "page")),
        P(),
        P(),
        P(),
        P(),
    )
    out_specs = (P(("row", "page"), None, "col"), P(None, ("row", "page"), None, "col"))
    return jax.shard_map(
        on_device, mesh=mesh, in_specs=in_specs, out_specs=out_specs, check_vma=False
    )
```

time: 524 us -> 321 us (0.61)
  waiting for transfers between devices: 333 us -> 218 us
  local copies, waits for them, and re-layouts: 82 us -> 13.8 us
  other arithmetic: 36 us -> 22.5 us
  matrix products: 46.5 us -> 39.8 us
    all_gather x7 -> x3, waiting for transfers between devices: 278 us -> 149 us  [gather_rows(): full = lax.all_gather(piece, ('row', 'page'), axis=0, tiled=True)]
    ppermute x0 -> x3, waiting for transfers between devices: none -> 61.6 us  [the longest x1 26.9 us: on_device(): attn_other = lax.ppermute(attn_terms, 'col', [(0, 1), (1, 0)])]
    reduce_scatter x2 -> x0, waiting for transfers between devices: 31.6 us -> none  [the longest x1 31.6 us: on_device(): lax.psum_scatter(attn_terms.astype(jnp.bfloat16), 'col', scatter_dimensio...]
    slice x4 -> x5, local copies, waits for them, and re-layouts: 30.5 us -> 4.57 us  [the longest x2 2.91 us: on_device(): projected[:, :, :local_width + kv_width]]
    gather x1 -> x2, local copies, waits for them, and re-layouts: 19.9 us -> 1.32 us  [the longest x1 0.72 us: on_device(): outgoing = jnp.take(both, from_block, axis=1)]
    squeeze x1 -> x2, local copies, waits for them, and re-layouts: 16.1 us -> 0.09 us  [the longest x1 0.09 us: on_device(): w_gateup[0]]
    all_to_all x1, waiting for transfers between devices: 22.5 us -> 7.62 us  [on_device(): lax.all_to_all(outgoing, 'page', split_axis=1, concat_axis=1, tiled=True)]
    convert_element_type x6 -> x2, other arithmetic: 14.3 us -> 4.32 us  [the longest x1 2.71 us: on_device(): (jax.nn.silu(gate_up[:, :unit_count]) * gate_up[:, unit_count:]).astype(b...]
  transfers between devices with their start and end apart: 10 -> 7, of which waited for: 7 -> 7; matrix products, arithmetic and copies ran while one was open for 27% -> 20% of each run, Pallas kernels for 0% -> 0%
where the time goes in v1:
time: 321 us; the launch traced here: 317 us
  waiting for transfers between devices  218 us (68%)
  matrix products  39.8 us (12%)
  other arithmetic  22.5 us (7%)
  between operations  14.8 us (5%)
  local copies, waits for them, and re-layouts  13.8 us (4%)
  starting transfers between devices  7.98 us (2%)
    all_gather x3, waiting for transfers between devices, gather_rows(): full = lax.all_gather(piece, ('row', 'page'), axis=0, tiled=True)  149 us
    ppermute x1, waiting for transfers between devices, on_device(): attn_other = lax.ppermute(attn_terms, 'col', [(0, 1), (1, 0)])  26.9 us
    ppermute x1, waiting for transfers between devices, gather_col(): other = lax.ppermute(values, 'col', [(0, 1), (1, 0)])  18.8 us
    ppermute x1, waiting for transfers between devices, on_device(): arrived = lax.ppermute(theirs, 'col', [(0, 1), (1, 0)])  15.9 us
    dot_general x1, matrix products, on_device(): jnp.dot(ffn_in.reshape(-1, model_width), gateup_full, preferred_element_t...  15 us
    all_to_all x1, waiting for transfers between devices, on_device(): lax.all_to_all(outgoing, 'page', split_axis=1, concat_axis=1, tiled=True)  7.62 us
  transfers between devices with their start and end apart: 7, of which 7 were waited for; matrix products, arithmetic and copies ran while one was open for 20% of the time, Pallas kernels for 0%

profile of v1, /device:TPU:17, one launch (start us, length us, event | category | flops | bytes accessed | tf_op | source)
XLA Modules:
  0.0 317.0 jit_solution(13522234820838018017)
XLA Ops:
  7.2 0.9 copy-done
  8.2 1.1 copy.35
  9.3 1.0 convert.33
  10.3 0.8 pad_maximum_fusion.3
  11.1 1.9 convert.39
  13.1 1.2 pad_maximum_fusion.1
  14.4 0.2 copy-done.3
  14.5 1.1 copy.41
  15.6 1.3 collective-permute-start
  16.9 0.2 convert_reduce_fusion
  17.2 0.7 iota_reduce_fusion.1
  18.5 0.6 pad_clamp_fusion.1
  19.2 1.0 fusion.42
  20.1 0.8 fusion.38
  20.9 18.8 %collective-permute-done = bf16[1,512,1024]{2,1,0:T(8,128)(2,1)S(1)} collective-permute-done((bf16[1,512,1024]{2,1,0:T(8,128)(2,1)S(1)}, bf16[1,512,1024]{2,1,0:T(8,128)(2,1)S(1)}, u32[]{:S(2)}, u32[]{:S(2)}) %collective-permute-start) | collective-permute-done | bytes 1048608 | tf_op jit(solution)/shard_map/ppermute | solution.py:50
  39.7 1.4 broadcast_select_fusion.1
  41.1 0.5 fusion.6
  41.6 26.6 %all-gather.4.cloned.1.call-done = bf16[2048,1280]{1,0:T(8,128)(2,1)} async-done(((bf16[128,1280]{1,0:T(8,128)(2,1)}), bf16[2048,1280]{1,0:T(8,128)(2,1)}) %all-gather.4.cloned.1.call-update) | async-done | bytes 5242896 | tf_op jit(solution)/shard_map/all_gather | solution.py:59
  68.2 3.7 %fusion.33 = f32[1,512,768]{2,1,0:T(8,128)S(1)} fusion(bf16[2048,1280]{1,0:T(8,128)(2,1)} %all-gather.4.cloned.1.call-done, bf16[512,1024]{1,0:T(8,128)(2,1)S(1)} %bitcast.86, bf16[512,1024]{1,0:T(8,128)(2,1)S(1)} %bitcast.85, f32[2048]{0:T(1024)S(1)} %copy-done.11, f32[512]{0:T(512)S(1)} %add_rsqrt_fusion.2), kind=kOutput, calls=%fused_computation.41 | convolution fusion | flops 1617952768 | bytes 6825984 | tf_op jit(solution)/shard_map/dot_general | solution.py:109
  71.9 1.2 slice.84
  73.1 1.7 copy.37
  74.9 0.8 copy.36
  75.6 0.2 multiply_reduce_fusion
  76.0 1.1 subtract_convert_fusion
  77.2 2.1 fusion
  79.3 2.3 fusion.37
  81.6 4.3 %fusion.14 = bf16[1,512,2048]{2,1,0:T(8,128)(2,1)} fusion(bf16[512,512]{0,1:T(8,128)(2,1)S(1)} %bitcast.92, bf16[2048,1280]{1,0:T(8,128)(2,1)} %all-gather.4.cloned.1.call-done), kind=kOutput, calls=%fused_computation.25 | convolution fusion | flops 1074790400 | bytes 4718592 | tf_op jit(solution)/shard_map/dot_general | solution.py:136
  85.9 1.2 collective-permute-start.1
  87.2 0.6 iota_reduce_fusion
  88.1 0.7 gather_fusion
  88.9 0.8 select_bitcast_fusion.1
  89.7 4.1 %all-to-all-start = ((bf16[2,4,128,128]{3,2,0,1:T(8,128)(2,1)}), bf16[2,4,128,128]{3,2,0,1:T(8,128)(2,1)S(1)}, u32[]{:S(2)}, u32[]{:S(2)}) async-start(bf16[2,4,128,128]{3,2,0,1:T(8,128)(2,1)} %select_bitcast_fusion.1), calls=%async_computation | async-start | bytes 524288 | tf_op jit(solution)/shard_map/all_to_all | solution.py:179
  93.8 7.6 %all-to-all-done = bf16[2,4,128,128]{3,2,0,1:T(8,128)(2,1)S(1)} async-done(((bf16[2,4,128,128]{3,2,0,1:T(8,128)(2,1)}), bf16[2,4,128,128]{3,2,0,1:T(8,128)(2,1)S(1)}, u32[]{:S(2)}, u32[]{:S(2)}) %all-to-all-start) | async-done | bytes 262176 | tf_op jit(solution)/shard_map/all_to_all | solution.py:179
  101.5 0.6 gather_fusion.1
  102.2 0.9 fusion.54
  103.1 3.2 %concatenate.60 = bf16[2,4,128,512]{3,2,0,1:T(8,128)(2,1)S(1)} concatenate(bf16[2,4,128,64]{3,2,0,1:T(8,128)(2,1)} %get-tuple-element.26, bf16[2,4,128,64]{3,2,0,1:T(8,128)(2,1)} %get-tuple-element.26, bf16[2,4,128,64]{3,2,0,1:T(8,128)(2,1)} %get-tuple-element.26, bf16[2,4,128,128]{3,2,0,1:T(8,128)(2,1)S(1)} %select_bitcast_fusion, bf16[2,4,128,64]{3,2,0,1:T(8,128)(2,1)} %get-tuple-element.25, ...), dimensions={3} | concatenate | bytes 2097152 | tf_op jit(solution)/shard_map/concatenate | solution.py:190
  106.3 26.9 %collective-permute-done.1 = bf16[1,512,2048]{2,1,0:T(8,128)(2,1)} collective-permute-done((bf16[1,512,2048]{2,1,0:T(8,128)(2,1)}, bf16[1,512,2048]{2,1,0:T(8,128)(2,1)}, u32[]{:S(2)}, u32[]{:S(2)}) %collective-permute-start.1) | collective-permute-done | bytes 2097184 | tf_op jit(solution)/shard_map/ppermute | solution.py:141
  133.1 4.9 %fusion.8 = (f32[512]{0:T(512)S(1)}, bf16[1,512,2048]{2,1,0:T(8,128)(2,1)}) fusion(bf16[1,512,2048]{2,1,0:T(8,128)(2,1)} %collective-permute-done.1, bf16[1,512,2048]{2,1,0:T(8,128)(2,1)} %fusion.14, bf16[1,512,1024]{2,1,0:T(8,128)(2,1)S(1)} %get-tuple-element.20, bf16[1,512,1024]{2,1,0:T(8,128)(2,1)S(1)} %get-tuple-element.19), kind=kLoop, calls=%fused_computation.17 | loop fusion | flops 12582400 | bytes 8390656 | tf_op jit(solution)/shard_map/reduce_sum | solution.py:11
  138.1 50.1 %all-gather.6.cloned.1.call-done = bf16[2048,5120]{1,0:T(8,128)(2,1)} async-done(((bf16[128,5120]{1,0:T(8,128)(2,1)}), bf16[2048,5120]{1,0:T(8,128)(2,1)}) %all-gather.6.cloned.1.call-update) | async-done | bytes 20971536 | tf_op jit(solution)/shard_map/all_gather | solution.py:59
  188.2 15.0 %fusion.16 = f32[512,5120]{1,0:T(8,128)S(1)} fusion(bf16[2048,5120]{1,0:T(8,128)(2,1)} %all-gather.6.cloned.1.call-done, bf16[1,512,2048]{2,1,0:T(8,128)(2,1)} %get-tuple-element.18, f32[2048]{0:T(1024)S(1)} %copy-done.12, f32[512]{0:T(512)S(1)} %add_rsqrt_fusion.1), kind=kOutput, calls=%fused_computation.27 | convolution fusion | flops 10741612544 | bytes 33564672 | tf_op jit(solution)/shard_map/dot_general | solution.py:200
  203.2 2.7 fusion.1
  205.9 72.2 %all-gather.8.cloned.1.call-done = bf16[2048,2560]{1,0:T(8,128)(2,1)} async-done(((bf16[128,2560]{1,0:T(8,128)(2,1)}), bf16[2048,2560]{1,0:T(8,128)(2,1)}) %all-gather.8.cloned.1.call-update) | async-done | bytes 10485776 | tf_op jit(solution)/shard_map/all_gather | solution.py:59
  278.1 6.2 %fusion.30 = bf16[512,1024]{1,0:T(8,128)(2,1)S(1)} fusion(bf16[512,2560]{1,0:T(8,128)(2,1)} %fusion.1, bf16[2048,2560]{1,0:T(8,128)(2,1)} %all-gather.8.cloned.1.call-done, s32[]{:T(128)S(6)} %select_n.90), kind=kOutput, calls=%fused_computation.40 | convolution fusion | flops 2684878848 | bytes 8912900 | tf_op jit(solution)/shard_map/dot_general | solution.py:209
  284.3 1.3 collective-permute-start.2
  285.6 6.3 %fusion.27 = bf16[512,1024]{1,0:T(8,128)(2,1)S(1)} fusion(bf16[512,2560]{1,0:T(8,128)(2,1)} %fusion.1, bf16[2048,2560]{1,0:T(8,128)(2,1)} %all-gather.8.cloned.1.call-done, s32[]{:T(128)S(6)} %select_n.84), kind=kOutput, calls=%fused_computation.39 | convolution fusion | flops 2684878848 | bytes 8912900 | tf_op jit(solution)/shard_map/dot_general | solution.py:213
  291.9 1.1 copy.42
  293.0 15.9 %collective-permute-done.2 = bf16[512,1024]{1,0:T(8,128)(2,1)S(1)} collective-permute-done((bf16[512,1024]{1,0:T(8,128)(2,1)S(1)}, bf16[512,1024]{1,0:T(8,128)(2,1)S(1)}, u32[]{:S(2)}, u32[]{:S(2)}) %collective-permute-start.2) | collective-permute-done | bytes 1048608 | tf_op jit(solution)/shard_map/ppermute | solution.py:212
  308.9 1.6 fusion.22
  (66 shorter events, 1.4 us)
Async XLA Ops:
  7.2 1.0 copy-start
  7.2 61.0 %all-gather.4.cloned.1.call-start = ((), (), s32[]{:S(2)}) async-start(), calls=%async_computation.1 | async-start | bytes 5570560 | tf_op jit(solution)/shard_map/all_gather | solution.py:59
  11.0 177.2 %all-gather.6.cloned.1.call-start = ((), (), s32[]{:S(2)}) async-start(), calls=%async_computation.2 | async-start | bytes 22282240 | tf_op jit(solution)/shard_map/all_gather | solution.py:59
  13.0 1.6 copy-start.3
  13.0 2.6 copy-start.4
  13.0 3.9 %copy-start.7 = (s32[4,4]{1,0:T(4,128)S(1)}, s32[4,4]{1,0:T(4,128)}, u32[]{:S(2)}) copy-start(s32[4,4]{1,0:T(4,128)} %param.16) | copy-start | bytes 196
  13.0 6.1 %copy-start.10 = (f32[64]{0:T(128)S(1)}, f32[64]{0:T(128)}, u32[]{:S(2)}) copy-start(f32[64]{0:T(128)} %param.24) | copy-start | bytes 772
  13.0 6.1 %copy-start.13 = (f32[64]{0:T(128)S(1)}, f32[64]{0:T(128)}, u32[]{:S(2)}) copy-start(f32[64]{0:T(128)} %param.25) | copy-start | bytes 772
  14.3 263.8 %all-gather.8.cloned.1.call-start = ((), (), s32[]{:S(2)}) async-start(), calls=%async_computation.3 | async-start | bytes 11141120 | tf_op jit(solution)/shard_map/all_gather | solution.py:59
  15.6 52.6 %copy-start.11 = (f32[2048]{0:T(1024)S(1)}, f32[2048]{0:T(1024)}, u32[]{:S(2)}) copy-start(f32[2048]{0:T(1024)} %param.22) | copy-start | bytes 24580
  15.6 24.1 %collective-permute-start = (bf16[1,512,1024]{2,1,0:T(8,128)(2,1)S(1)}, bf16[1,512,1024]{2,1,0:T(8,128)(2,1)S(1)}, u32[]{:S(2)}, u32[]{:S(2)}) collective-permute-start(bf16[1,512,1024]{2,1,0:T(8,128)(2,1)S(1)} %copy-done.4), channel_id=1, source_target_pairs={{0,4},{4,0},{1,5},{5,1},{2,6},{6,2},{3,7},{7,3},{8,12},{12,8},{9,1... | collective-permute-start | bytes 3145736 | tf_op jit(solution)/shard_map/ppermute | solution.py:50
  17.8 54.1 %copy-start.14 = (s32[4]{0:T(128)}, s32[4]{0:T(128)S(1)}, u32[]{:S(2)}) copy-start(s32[4]{0:T(128)S(1)} %get-tuple-element.7) | copy-start | bytes 52
  18.5 53.4 %copy-start.8 = (pred[512]{0:T(512)(128)(4,1)}, pred[512]{0:T(512)(128)(4,1)S(1)}, u32[]{:S(2)}) copy-start(pred[512]{0:T(512)(128)(4,1)S(1)} %iota_compare_fusion.4) | copy-start | bytes 1540
  75.6 1.5 copy-start.5
  77.2 2.1 copy-start.6
  77.2 2.1 copy-start.9
  81.6 5.6 %copy-start.15 = (s32[4]{0:T(128)S(1)}, s32[4]{0:T(128)}, u32[]{:S(2)}) copy-start(s32[4]{0:T(128)} %copy-done.14) | copy-start | bytes 52
  85.9 47.3 %collective-permute-start.1 = (bf16[1,512,2048]{2,1,0:T(8,128)(2,1)}, bf16[1,512,2048]{2,1,0:T(8,128)(2,1)}, u32[]{:S(2)}, u32[]{:S(2)}) collective-permute-start(bf16[1,512,2048]{2,1,0:T(8,128)(2,1)} %fusion.14), channel_id=1, source_target_pairs={{0,4},{4,0},{1,5},{5,1},{2,6},{6,2},{3,7},{7,3},{8,12},{12,8},{9,1... | collective-permute-start | bytes 6291464 | tf_op jit(solution)/shard_map/ppermute | solution.py:141
  89.7 11.8 %all-to-all-start = ((bf16[2,4,128,128]{3,2,0,1:T(8,128)(2,1)}), bf16[2,4,128,128]{3,2,0,1:T(8,128)(2,1)S(1)}, u32[]{:S(2)}, u32[]{:S(2)}) async-start(bf16[2,4,128,128]{3,2,0,1:T(8,128)(2,1)} %select_bitcast_fusion.1), calls=%async_computation | async-start | bytes 524288 | tf_op jit(solution)/shard_map/all_to_all | solution.py:179
  106.3 82.0 %copy-start.12 = (f32[2048]{0:T(1024)S(1)}, f32[2048]{0:T(1024)}, u32[]{:S(2)}) copy-start(f32[2048]{0:T(1024)} %param.23) | copy-start | bytes 24580
  284.3 24.6 %collective-permute-start.2 = (bf16[512,1024]{1,0:T(8,128)(2,1)S(1)}, bf16[512,1024]{1,0:T(8,128)(2,1)S(1)}, u32[]{:S(2)}, u32[]{:S(2)}) collective-permute-start(bf16[512,1024]{1,0:T(8,128)(2,1)S(1)} %fusion.30), channel_id=1, source_target_pairs={{0,4},{4,0},{1,5},{5,1},{2,6},{6,2},{3,7},{7,3},{8,12},{12,8},{9,1... | collective-permute-start | bytes 3145736 | tf_op jit(solution)/shard_map/ppermute | solution.py:212
  285.6 23.3 %copy-start.2 = (bf16[1,512,2048]{2,1,0:T(8,128)(2,1)S(1)}, bf16[1,512,2048]{2,1,0:T(8,128)(2,1)}, u32[]{:S(2)}) copy-start(bf16[1,512,2048]{2,1,0:T(8,128)(2,1)} %get-tuple-element.18) | copy-start | bytes 6291460
  285.6 24.9 %copy-start.1 = (f32[2,128,256]{2,1,0:T(8,128)S(1)}, f32[2,128,256]{2,1,0:T(8,128)}, u32[]{:S(2)}) copy-start(f32[2,128,256]{2,1,0:T(8,128)} %param.18) | copy-start | bytes 786436
Sparse Core Ops, SparseCore 0:
  11.2 56.9 all-gather.3
  69.7 118.4 all-gather.5
  191.1 86.9 all-gather.7

commit v2 on v1

--- a/solution.py
+++ b/solution.py
@@ -97,11 +97,11 @@
     attn_piece = jnp.concatenate(
         [w_query, keyval_piece[0], keyval_piece[1], w_out.T], axis=1
     ).astype(bf16)
-    gateup_piece = jnp.concatenate([w_gateup[0], w_gateup[1]], axis=1).astype(bf16)
-    down_piece = w_down.T.astype(bf16)
+    ffn_piece = jnp.concatenate([w_gateup[0], w_gateup[1], w_down.T], axis=1).astype(bf16)
     attn_full = gather_rows(attn_piece)
-    gateup_full = gather_rows(gateup_piece)
-    down_full = gather_rows(down_piece)
+    ffn_full = gather_rows(ffn_piece)
+    gateup_full = ffn_full[:, : 2 * unit_count]
+    down_full = ffn_full[:, 2 * unit_count :]
     qkv_width = local_width + 2 * kv_width
     out_t = attn_full[:, qkv_width:]
 
@@ -197,30 +197,39 @@
     )
 
     ffn_in = normalize(residual_all.astype(f32), ffn_gain).astype(bf16)
-    gate_up = jnp.dot(
-        ffn_in.reshape(-1, model_width), gateup_full, preferred_element_type=f32
-    )
-    hidden = (jax.nn.silu(gate_up[:, :unit_count]) * gate_up[:, unit_count:]).astype(bf16)
-    kv_pages, hidden = lax.optimization_barrier((kv_pages, hidden))
+    ffn_in = ffn_in.reshape(-1, model_width)
+    kv_pages, ffn_in = lax.optimization_barrier((kv_pages, ffn_in))
     contract_last = (((1,), (1,)), ((), ()))
+
+    def hidden_of(rows):
+        gate_up = jnp.dot(rows, gateup_full, preferred_element_type=f32)
+        return (jax.nn.silu(gate_up[:, :unit_count]) * gate_up[:, unit_count:]).astype(bf16)
+
+    def down_terms(hidden, weights):
+        return lax.dot_general(
+            hidden, weights, contract_last, preferred_element_type=f32
+        ).astype(bf16)
+
     if col_count == 2:
         other_w = lax.dynamic_slice_in_dim(down_full, (1 - col_index) * local_feat, local_feat, 0)
         own_w = lax.dynamic_slice_in_dim(down_full, col_index * local_feat, local_feat, 0)
-        theirs = lax.dot_general(
-            hidden, other_w, contract_last, preferred_element_type=f32
-        ).astype(bf16)
-        arrived = lax.ppermute(theirs, "col", [(0, 1), (1, 0)])
-        mine = lax.dot_general(
-            hidden, own_w, contract_last, preferred_element_type=f32
-        ).astype(bf16)
-        mine = lax.optimization_barrier(mine)
+        first_in, second_in = jnp.split(ffn_in, 2)
+        first_hidden = hidden_of(first_in)
+        first_theirs = down_terms(first_hidden, other_w)
+        first_arrived = lax.ppermute(first_theirs, "col", [(0, 1), (1, 0)])
+        second_in, first_theirs = lax.optimization_barrier((second_in, first_theirs))
+        second_hidden = hidden_of(second_in)
+        second_theirs = down_terms(second_hidden, other_w)
+        second_arrived = lax.ppermute(second_theirs, "col", [(0, 1), (1, 0)])
+        hidden = jnp.concatenate([first_hidden, second_hidden])
+        hidden, second_theirs = lax.optimization_barrier((hidden, second_theirs))
+        mine = lax.optimization_barrier(down_terms(hidden, own_w))
+        arrived = jnp.concatenate([first_arrived, second_arrived])
         ffn_sum = (mine.astype(f32) + arrived.astype(f32)).reshape(
             prompt_count, seq_len, local_feat
         )
     else:
-        ffn_terms = lax.dot_general(
-            hidden, down_full, contract_last, preferred_element_type=f32
-        ).astype(bf16)
+        ffn_terms = down_terms(hidden_of(ffn_in), down_full)
         ffn_sum = lax.psum_scatter(
             ffn_terms.reshape(prompt_count, seq_len, model_width),
             "col",

time: 321 us -> 314 us (0.978); the launches traced: 317 us -> 314 us
  waiting for transfers between devices: 218 us -> 205 us
  local copies, waits for them, and re-layouts: 13.8 us -> 24.4 us
  other arithmetic: 22.5 us -> 18.5 us
    all_gather x3 -> x2, waiting for transfers between devices: 149 us -> 129 us  [gather_rows(): full = lax.all_gather(piece, ('row', 'page'), axis=0, tiled=True)]
    slice x0 -> x1, local copies, waits for them, and re-layouts: none -> 8.48 us  [on_device(): down_full = ffn_full[:, 2 * unit_count:]]
    ppermute x1 -> x2, waiting for transfers between devices: 15.9 us -> 20.5 us  [the longest x1 20.5 us: on_device(): second_arrived = lax.ppermute(second_theirs, 'col', [(0, 1), (1, 0)])]
    unnamed x35 -> x41, local copies, waits for them, and re-layouts: 4.34 us -> 7.53 us
    dot_general x3 -> x5, matrix products: 27.5 us -> 30.2 us  [the longest x2 20.4 us: hidden_of(): gate_up = jnp.dot(rows, gateup_full, preferred_element_type=f32)]
  transfers between devices with their start and end apart: 7 -> 7, of which waited for: 7 -> 6; matrix products, arithmetic and copies ran while one was open for 20% -> 12% of each run, Pallas kernels for 0% -> 0%
where the time goes in v2:
time: 314 us
  waiting for transfers between devices  205 us (65%)
  matrix products  42.5 us (14%)
  local copies, waits for them, and re-layouts  24.4 us (8%)
  other arithmetic  18.5 us (6%)
  between operations  15.2 us (5%)
  starting transfers between devices  8.11 us (3%)
    all_gather x2, waiting for transfers between devices, gather_rows(): full = lax.all_gather(piece, ('row', 'page'), axis=0, tiled=True)  129 us
    ppermute x1, waiting for transfers between devices, on_device(): attn_other = lax.ppermute(attn_terms, 'col', [(0, 1), (1, 0)])  27.4 us
    ppermute x1, waiting for transfers between devices, on_device(): second_arrived = lax.ppermute(second_theirs, 'col', [(0, 1), (1, 0)])  20.5 us
    dot_general x2, matrix products, hidden_of(): gate_up = jnp.dot(rows, gateup_full, preferred_element_type=f32)  20.4 us
    ppermute x1, waiting for transfers between devices, gather_col(): other = lax.ppermute(values, 'col', [(0, 1), (1, 0)])  20.1 us
    dot_general x3, matrix products, down_terms(): lax.dot_general(hidden, weights, contract_last, preferred_element_type=f32)  9.82 us
    slice x1, local copies, waits for them, and re-layouts, on_device(): down_full = ffn_full[:, 2 * unit_count:]  8.48 us
    all_to_all x1, waiting for transfers between devices, on_device(): lax.all_to_all(outgoing, 'page', split_axis=1, concat_axis=1, tiled=True)  7.61 us
  transfers between devices with their start and end apart: 7, of which 6 were waited for; matrix products, arithmetic and copies ran while one was open for 12% of the time, Pallas kernels for 0%

profile of v2, /device:TPU:17, one launch (start us, length us, event | category | flops | bytes accessed | tf_op | source)
XLA Modules:
  0.0 313.8 jit_solution(7133177114508803366)
XLA Ops:
  7.3 0.9 copy-done
  8.2 1.0 convert.37
  9.2 1.1 copy.35
  10.3 0.8 pad_maximum_fusion.4
  11.1 1.6 copy.41
  12.9 1.4 pad_maximum_fusion.2
  14.4 1.2 collective-permute-start
  15.9 0.6 iota_reduce_fusion.1
  17.3 0.3 fusion.49
  17.6 0.8 fusion.45
  18.5 20.1 %collective-permute-done = bf16[1,512,1024]{2,1,0:T(8,128)(2,1)} collective-permute-done((bf16[1,512,1024]{2,1,0:T(8,128)(2,1)S(1)}, bf16[1,512,1024]{2,1,0:T(8,128)(2,1)}, u32[]{:S(2)}, u32[]{:S(2)}) %collective-permute-start) | collective-permute-done | bytes 1048608 | tf_op jit(solution)/shard_map/ppermute | solution.py:50
  38.6 1.4 broadcast_select_fusion.1
  40.0 0.5 fusion.11
  40.5 27.7 %all-gather.3.cloned.1.call-done = bf16[2048,1280]{1,0:T(8,128)(2,1)} async-done(((bf16[128,1280]{1,0:T(8,128)(2,1)}), bf16[2048,1280]{1,0:T(8,128)(2,1)}) %all-gather.3.cloned.1.call-update) | async-done | bytes 5242896 | tf_op jit(solution)/shard_map/all_gather | solution.py:59
  68.2 3.7 %fusion.33 = f32[1,512,768]{2,1,0:T(8,128)S(1)} fusion(bf16[2048,1280]{1,0:T(8,128)(2,1)} %all-gather.3.cloned.1.call-done, bf16[512,1024]{1,0:T(8,128)(2,1)S(1)} %bitcast.88, bf16[512,1024]{1,0:T(8,128)(2,1)S(1)} %bitcast.87, f32[2048]{0:T(1024)S(1)} %copy-done.14, f32[512]{0:T(512)S(1)} %add_rsqrt_fusion.2), kind=kOutput, calls=%fused_computation.47 | convolution fusion | flops 1617952768 | bytes 6825984 | tf_op jit(solution)/shard_map/dot_general | solution.py:109
  71.9 1.2 slice.100
  73.1 1.7 copy.37
  75.7 0.7 copy-done.9
  76.3 2.1 fusion.4
  78.4 2.3 fusion.43
  80.7 4.3 %fusion.19 = bf16[1,512,2048]{2,1,0:T(8,128)(2,1)} fusion(bf16[512,512]{0,1:T(8,128)(2,1)S(1)} %bitcast.94, bf16[2048,1280]{1,0:T(8,128)(2,1)} %all-gather.3.cloned.1.call-done), kind=kOutput, calls=%fused_computation.29 | convolution fusion | flops 1074790400 | bytes 4718592 | tf_op jit(solution)/shard_map/dot_general | solution.py:136
  84.9 1.2 collective-permute-start.1
  86.3 0.6 iota_reduce_fusion
  87.2 0.6 gather_fusion
  87.8 0.8 select_bitcast_fusion.1
  88.6 4.1 %all-to-all-start = ((bf16[2,4,128,128]{3,2,0,1:T(8,128)(2,1)}), bf16[2,4,128,128]{3,2,0,1:T(8,128)(2,1)S(1)}, u32[]{:S(2)}, u32[]{:S(2)}) async-start(bf16[2,4,128,128]{3,2,0,1:T(8,128)(2,1)} %select_bitcast_fusion.1), calls=%async_computation | async-start | bytes 524288 | tf_op jit(solution)/shard_map/all_to_all | solution.py:179
  92.8 7.6 %all-to-all-done = bf16[2,4,128,128]{3,2,0,1:T(8,128)(2,1)S(1)} async-done(((bf16[2,4,128,128]{3,2,0,1:T(8,128)(2,1)}), bf16[2,4,128,128]{3,2,0,1:T(8,128)(2,1)S(1)}, u32[]{:S(2)}, u32[]{:S(2)}) %all-to-all-start) | async-done | bytes 262176 | tf_op jit(solution)/shard_map/all_to_all | solution.py:179
  100.4 0.6 gather_fusion.1
  101.3 3.6 %concatenate.66 = bf16[2,4,128,512]{3,2,0,1:T(8,128)(2,1)} concatenate(bf16[2,4,128,64]{3,2,0,1:T(8,128)(2,1)S(1)} %get-tuple-element.30, bf16[2,4,128,64]{3,2,0,1:T(8,128)(2,1)S(1)} %get-tuple-element.30, bf16[2,4,128,64]{3,2,0,1:T(8,128)(2,1)S(1)} %get-tuple-element.30, bf16[2,4,128,128]{3,2,0,1:T(8,128)(2,1)S(1)} %select_bitcast_fusion, ...), dimensions={3} | concatenate | bytes 2097152 | tf_op jit(solution)/shard_map/concatenate | solution.py:190
  104.9 27.4 %collective-permute-done.1 = bf16[1,512,2048]{2,1,0:T(8,128)(2,1)} collective-permute-done((bf16[1,512,2048]{2,1,0:T(8,128)(2,1)}, bf16[1,512,2048]{2,1,0:T(8,128)(2,1)}, u32[]{:S(2)}, u32[]{:S(2)}) %collective-permute-start.1) | collective-permute-done | bytes 2097184 | tf_op jit(solution)/shard_map/ppermute | solution.py:141
  132.2 3.9 %fusion.13 = (f32[512]{0:T(512)S(1)}, bf16[1,512,2048]{2,1,0:T(8,128)(2,1)S(1)}) fusion(bf16[1,512,2048]{2,1,0:T(8,128)(2,1)} %collective-permute-done.1, bf16[1,512,2048]{2,1,0:T(8,128)(2,1)} %fusion.19, bf16[1,512,1024]{2,1,0:T(8,128)(2,1)} %copy-done.2, bf16[1,512,1024]{2,1,0:T(8,128)(2,1)S(1)} %get-tuple-element.23), kind=kLoop, calls=%fused_computation.21 | loop fusion | flops 12582400 | bytes 8390656 | tf_op jit(solution)/shard_map/reduce_sum | solution.py:11
  136.1 0.5 fusion.22
  136.7 0.7 copy-done.5
  137.4 1.1 copy.42
  138.5 0.6 copy-done.4
  139.1 101.8 %all-gather.5.cloned.1.call-done = bf16[2048,7680]{1,0:T(8,128)(2,1)} async-done(((bf16[128,7680]{1,0:T(8,128)(2,1)}), bf16[2048,7680]{1,0:T(8,128)(2,1)}) %all-gather.5.cloned.1.call-update) | async-done | bytes 31457296 | tf_op jit(solution)/shard_map/all_gather | solution.py:59
  240.9 10.1 %fusion.2 = f32[256,5120]{1,0:T(8,128)S(1)} fusion(bf16[2048,7680]{1,0:T(8,128)(2,1)} %all-gather.5.cloned.1.call-done, bf16[512,2048]{1,0:T(8,128)(2,1)} %copy-done.4), kind=kOutput, calls=%fused_computation.4 | convolution fusion | flops 5368709120 | bytes 27262976 | tf_op jit(solution)/shard_map/dot_general | solution.py:205
  251.0 1.8 fusion.21
  252.9 8.5 %slice.111 = bf16[2048,2560]{1,0:T(8,128)(2,1)} slice(bf16[2048,7680]{1,0:T(8,128)(2,1)} %all-gather.5.cloned.1.call-done), slice={[0:2048], [5120:7680]} | slice | bytes 20971520 | tf_op jit(solution)/shard_map/slice | solution.py:104
  261.4 5.4 %fusion.36 = bf16[256,1024]{1,0:T(8,128)(2,1)} fusion(bf16[256,2560]{1,0:T(8,128)(2,1)} %fusion.21, bf16[2048,2560]{1,0:T(8,128)(2,1)} %slice.111, s32[]{:T(128)S(6)} %select_n.90), kind=kOutput, calls=%fused_computation.50 | convolution fusion | flops 1342439424 | bytes 7077892 | tf_op jit(solution)/shard_map/dot_general | solution.py:209
  266.7 10.2 %fusion = f32[256,5120]{1,0:T(8,128)S(1)} fusion(bf16[256,2048]{1,0:T(8,128)(2,1)S(1)} %slice-done.3, bf16[2048,7680]{1,0:T(8,128)(2,1)} %all-gather.5.cloned.1.call-done), kind=kOutput, calls=%fused_computation.2 | convolution fusion | flops 5368709120 | bytes 27262976 | tf_op jit(solution)/shard_map/dot_general | solution.py:205
  277.0 0.8 fusion.20
  277.8 1.6 fusion.39
  279.6 0.9 copy-done.13
  280.4 1.2 collective-permute-start.2
  281.9 2.9 fusion.30
  284.8 20.5 %collective-permute-done.3 = bf16[256,1024]{1,0:T(8,128)(2,1)S(1)} collective-permute-done((bf16[256,1024]{1,0:T(8,128)(2,1)S(1)}, bf16[256,1024]{1,0:T(8,128)(2,1)S(1)}, u32[]{:S(2)}, u32[]{:S(2)}) %collective-permute-start.3) | collective-permute-done | bytes 524320 | tf_op jit(solution)/shard_map/ppermute | solution.py:223
  305.3 1.6 fusion.27
  (80 shorter events, 2.8 us)
Async XLA Ops:
  7.2 1.0 copy-start
  7.2 5.5 %copy-start.6 = (f32[2,128,2560]{2,1,0:T(8,128)S(1)}, f32[2,128,2560]{2,1,0:T(8,128)}, u32[]{:S(2)}) copy-start(f32[2,128,2560]{2,1,0:T(8,128)} %param.20) | copy-start | bytes 7864324
  7.2 61.0 %all-gather.3.cloned.1.call-start = ((), (), s32[]{:S(2)}) async-start(), calls=%async_computation.1 | async-start | bytes 5570560 | tf_op jit(solution)/shard_map/all_gather | solution.py:59
  11.0 229.8 %all-gather.5.cloned.1.call-start = ((), (), s32[]{:S(2)}) async-start(), calls=%async_computation.2 | async-start | bytes 33423360 | tf_op jit(solution)/shard_map/all_gather | solution.py:59
  12.9 1.5 copy-start.7
  12.9 2.8 copy-start.11
  12.9 4.3 %copy-start.15 = (f32[64]{0:T(128)S(1)}, f32[64]{0:T(128)}, u32[]{:S(2)}) copy-start(f32[64]{0:T(128)} %param.25) | copy-start | bytes 772
  12.9 4.4 %copy-start.12 = (f32[64]{0:T(128)S(1)}, f32[64]{0:T(128)}, u32[]{:S(2)}) copy-start(f32[64]{0:T(128)} %param.24) | copy-start | bytes 772
  14.4 24.2 %copy-start.8 = (bf16[1,512,1024]{2,1,0:T(8,128)(2,1)S(1)}, bf16[1,512,1024]{2,1,0:T(8,128)(2,1)}, u32[]{:S(2)}) copy-start(bf16[1,512,1024]{2,1,0:T(8,128)(2,1)} %param.14) | copy-start | bytes 3145732
  14.4 24.2 %collective-permute-start = (bf16[1,512,1024]{2,1,0:T(8,128)(2,1)S(1)}, bf16[1,512,1024]{2,1,0:T(8,128)(2,1)}, u32[]{:S(2)}, u32[]{:S(2)}) collective-permute-start(bf16[1,512,1024]{2,1,0:T(8,128)(2,1)S(1)} %copy-done.7), channel_id=1, source_target_pairs={{0,4},{4,0},{1,5},{5,1},{2,6},{6,2},{3,7},{7,3},{8,12},{12,8},{9,1... | collective-permute-start | bytes 3145736 | tf_op jit(solution)/shard_map/ppermute | solution.py:50
  18.5 49.7 %copy-start.14 = (f32[2048]{0:T(1024)S(1)}, f32[2048]{0:T(1024)}, u32[]{:S(2)}) copy-start(f32[2048]{0:T(1024)} %param.22) | copy-start | bytes 24580
  40.0 31.9 %copy-start.2 = (bf16[1,512,1024]{2,1,0:T(8,128)(2,1)}, bf16[1,512,1024]{2,1,0:T(8,128)(2,1)S(1)}, u32[]{:S(2)}) copy-start(bf16[1,512,1024]{2,1,0:T(8,128)(2,1)S(1)} %get-tuple-element.24) | copy-start | bytes 3145732
  75.4 1.0 copy-start.9
  84.9 47.3 %collective-permute-start.1 = (bf16[1,512,2048]{2,1,0:T(8,128)(2,1)}, bf16[1,512,2048]{2,1,0:T(8,128)(2,1)}, u32[]{:S(2)}, u32[]{:S(2)}) collective-permute-start(bf16[1,512,2048]{2,1,0:T(8,128)(2,1)} %fusion.19), channel_id=1, source_target_pairs={{0,4},{4,0},{1,5},{5,1},{2,6},{6,2},{3,7},{7,3},{8,12},{12,8},{9,1... | collective-permute-start | bytes 6291464 | tf_op jit(solution)/shard_map/ppermute | solution.py:141
  88.6 11.8 %all-to-all-start = ((bf16[2,4,128,128]{3,2,0,1:T(8,128)(2,1)}), bf16[2,4,128,128]{3,2,0,1:T(8,128)(2,1)S(1)}, u32[]{:S(2)}, u32[]{:S(2)}) async-start(bf16[2,4,128,128]{3,2,0,1:T(8,128)(2,1)} %select_bitcast_fusion.1), calls=%async_computation | async-start | bytes 524288 | tf_op jit(solution)/shard_map/all_to_all | solution.py:179
  104.9 31.3 %copy-start.10 = (f32[2048]{0:T(1024)S(1)}, f32[2048]{0:T(1024)}, u32[]{:S(2)}) copy-start(f32[2048]{0:T(1024)} %param.23) | copy-start | bytes 24580
  136.1 1.2 copy-start.5
  137.3 1.7 copy-start.4
  261.3 5.4 %slice-start.3 = ((bf16[512,2048]{1,0:T(8,128)(2,1)}), bf16[256,2048]{1,0:T(8,128)(2,1)S(1)}, s32[]{:S(2)}) async-start(bf16[512,2048]{1,0:T(8,128)(2,1)} %copy-done.4), calls=%async_computation.6 | async-start | bytes 2097152 | tf_op jit(solution)/shard_map/split | solution.py:216
  261.4 16.4 %slice-start = ((s8[10485760]{0:T(1024)(128)(4,1)}), s8[4194304]{0:T(1024)(128)(4,1)S(1)}, s32[]{:S(2)}) async-start(s8[10485760]{0:T(1024)(128)(4,1)} %bitcast.85), calls=%async_computation.3 | async-start | bytes 8388608
  266.7 11.0 %slice-start.1 = ((s8[10485760]{0:T(1024)(128)(4,1)}), s8[4194304]{0:T(1024)(128)(4,1)S(1)}, s32[]{:S(2)}) async-start(s8[10485760]{0:T(1024)(128)(4,1)} %bitcast.85), calls=%async_computation.4 | async-start | bytes 8388608
  266.7 11.1 %slice-start.2 = ((s8[10485760]{0:T(1024)(128)(4,1)}), s8[2097152]{0:T(1024)(128)(4,1)S(1)}, s32[]{:S(2)}) async-start(s8[10485760]{0:T(1024)(128)(4,1)} %bitcast.85), calls=%async_computation.5 | async-start | bytes 4194304
  277.8 1.6 copy-start.3
  279.4 1.0 copy-start.13
  280.4 24.9 %collective-permute-start.2 = (bf16[256,1024]{1,0:T(8,128)(2,1)S(1)}, bf16[256,1024]{1,0:T(8,128)(2,1)S(1)}, u32[]{:S(2)}, u32[]{:S(2)}) collective-permute-start(bf16[256,1024]{1,0:T(8,128)(2,1)S(1)} %copy-done.13), channel_id=1, source_target_pairs={{0,4},{4,0},{1,5},{5,1},{2,6},{6,2},{3,7},{7,3},{8,12},{12,8},{9,1... | collective-permute-start | bytes 1572872 | tf_op jit(solution)/shard_map/ppermute | solution.py:219
  281.6 23.7 %collective-permute-start.3 = (bf16[256,1024]{1,0:T(8,128)(2,1)S(1)}, bf16[256,1024]{1,0:T(8,128)(2,1)S(1)}, u32[]{:S(2)}, u32[]{:S(2)}) collective-permute-start(bf16[256,1024]{1,0:T(8,128)(2,1)S(1)} %fusion.39), channel_id=1, source_target_pairs={{0,4},{4,0},{1,5},{5,1},{2,6},{6,2},{3,7},{7,3},{8,12},{12,8},{9,1... | collective-permute-start | bytes 1572872 | tf_op jit(solution)/shard_map/ppermute | solution.py:223
  281.9 25.1 %copy-start.1 = (f32[2,128,256]{2,1,0:T(8,128)S(1)}, f32[2,128,256]{2,1,0:T(8,128)}, u32[]{:S(2)}) copy-start(f32[2,128,256]{2,1,0:T(8,128)} %param.18) | copy-start | bytes 786436
Sparse Core Ops, SparseCore 0:
  11.2 56.9 all-gather.2
  69.7 171.1 all-gather.4

commit v3 on v2

--- a/solution.py
+++ b/solution.py
@@ -58,6 +58,37 @@
     piece = with_layout_constraint(piece, rows_major)
     full = lax.all_gather(piece, ("row", "page"), axis=0, tiled=True)
     return with_layout_constraint(full, rows_major)
+
+
+def exchange(values, axis, bit):
+    count = lax.axis_size(axis)
+    return lax.ppermute(values, axis, [(i, i ^ bit) for i in range(count)])
+
+
+def gather_doubling(piece):
+    row_count = lax.axis_size("row")
+    page_count = lax.axis_size("page")
+    if row_count & (row_count - 1) or page_count & (page_count - 1):
+        return gather_rows(piece)
+    held = piece[None]
+    bit = 1
+    while bit < page_count:
+        other = exchange(held, "page", bit)
+        upper = (lax.axis_index("page") & bit) != 0
+        held = jnp.concatenate(
+            [jnp.where(upper, other, held), jnp.where(upper, held, other)], axis=0
+        )
+        bit *= 2
+    held = held[None]
+    bit = row_count // 2
+    while bit >= 1:
+        other = exchange(held, "row", bit)
+        upper = (lax.axis_index("row") & bit) != 0
+        held = jnp.stack(
+            [jnp.where(upper, other, held), jnp.where(upper, held, other)], axis=1
+        ).reshape(2 * held.shape[0], *held.shape[1:])
+        bit //= 2
+    return held.reshape(-1, piece.shape[1])
 
 
 def on_device(
@@ -98,10 +129,9 @@
         [w_query, keyval_piece[0], keyval_piece[1], w_out.T], axis=1
     ).astype(bf16)
     ffn_piece = jnp.concatenate([w_gateup[0], w_gateup[1], w_down.T], axis=1).astype(bf16)
-    attn_full = gather_rows(attn_piece)
     ffn_full = gather_rows(ffn_piece)
+    attn_full = gather_doubling(attn_piece)
     gateup_full = ffn_full[:, : 2 * unit_count]
-    down_full = ffn_full[:, 2 * unit_count :]
     qkv_width = local_width + 2 * kv_width
     out_t = attn_full[:, qkv_width:]
 
@@ -211,25 +241,18 @@
         ).astype(bf16)
 
     if col_count == 2:
-        other_w = lax.dynamic_slice_in_dim(down_full, (1 - col_index) * local_feat, local_feat, 0)
-        own_w = lax.dynamic_slice_in_dim(down_full, col_index * local_feat, local_feat, 0)
-        first_in, second_in = jnp.split(ffn_in, 2)
-        first_hidden = hidden_of(first_in)
-        first_theirs = down_terms(first_hidden, other_w)
-        first_arrived = lax.ppermute(first_theirs, "col", [(0, 1), (1, 0)])
-        second_in, first_theirs = lax.optimization_barrier((second_in, first_theirs))
-        second_hidden = hidden_of(second_in)
-        second_theirs = down_terms(second_hidden, other_w)
-        second_arrived = lax.ppermute(second_theirs, "col", [(0, 1), (1, 0)])
-        hidden = jnp.concatenate([first_hidden, second_hidden])
-        hidden, second_theirs = lax.optimization_barrier((hidden, second_theirs))
-        mine = lax.optimization_barrier(down_terms(hidden, own_w))
-        arrived = jnp.concatenate([first_arrived, second_arrived])
+        down_at = lambda col: lax.dynamic_slice(
+            ffn_full, (col * local_feat, 2 * unit_count), (local_feat, unit_count)
+        )
+        hidden = hidden_of(ffn_in)
+        theirs = down_terms(hidden, down_at(1 - col_index))
+        arrived = lax.ppermute(theirs, "col", [(0, 1), (1, 0)])
+        mine = lax.optimization_barrier(down_terms(hidden, down_at(col_index)))
         ffn_sum = (mine.astype(f32) + arrived.astype(f32)).reshape(
             prompt_count, seq_len, local_feat
         )
     else:
-        ffn_terms = down_terms(hidden_of(ffn_in), down_full)
+        ffn_terms = down_terms(hidden_of(ffn_in), ffn_full[:, 2 * unit_count :])
         ffn_sum = lax.psum_scatter(
             ffn_terms.reshape(prompt_count, seq_len, model_width),
             "col",

time: 314 us -> 273 us (0.87)
  waiting for transfers between devices: 205 us -> 143 us
  starting transfers between devices: 8.11 us -> 31.3 us
  local copies, waits for them, and re-layouts: 24.4 us -> 8.7 us
  other arithmetic: 18.5 us -> 29.5 us
    all_gather x2 -> x1, waiting for transfers between devices: 129 us -> 26.7 us  [gather_rows(): full = lax.all_gather(piece, ('row', 'page'), axis=0, tiled=True)]
    ppermute x2 -> x5, waiting for transfers between devices: 20.5 us -> 78.4 us  [the longest x4 70 us: exchange(): return lax.ppermute(values, axis, [(i, i ^ bit) for i in range(count)])]
    all_to_all x1, starting transfers between devices: 4.11 us -> 22.8 us  [on_device(): lax.all_to_all(outgoing, 'page', split_axis=1, concat_axis=1, tiled=True)]
    ppermute x1, waiting for transfers between devices: 27.4 us -> 9.08 us  [on_device(): attn_other = lax.ppermute(attn_terms, 'col', [(0, 1), (1, 0)])]
    slice x1, local copies, waits for them, and re-layouts: 8.48 us -> 0.01 us  [on_device(): keyval_piece[0]]
    another operation x3 -> x5, other arithmetic: 1.3 us -> 6.66 us  [the longest x3 4.48 us: gather_doubling(): jnp.stack([jnp.where(upper, other, held), jnp.where(upper, held, other)],...]
    ppermute x2 -> x5, starting transfers between devices: 1.48 us -> 6.51 us  [the longest x4 5.32 us: exchange(): return lax.ppermute(values, axis, [(i, i ^ bit) for i in range(count)])]
    unnamed x41 -> x37, local copies, waits for them, and re-layouts: 7.53 us -> 2.74 us
  transfers between devices with their start and end apart: 7 -> 9, of which waited for: 6 -> 8; matrix products, arithmetic and copies ran while one was open for 12% -> 16% of each run, Pallas kernels for 0% -> 0%
where the time goes in v3:
time: 273 us; the launch traced here: 270 us
  waiting for transfers between devices  143 us (52%)
  matrix products  42 us (15%)
  starting transfers between devices  31.3 us (11%)
  other arithmetic  29.5 us (11%)
  between operations  15.2 us (6%)
  local copies, waits for them, and re-layouts  8.7 us (3%)
    ppermute x4, waiting for transfers between devices, exchange(): return lax.ppermute(values, axis, [(i, i ^ bit) for i in range(count)])  70 us
    all_gather x1, waiting for transfers between devices, gather_rows(): full = lax.all_gather(piece, ('row', 'page'), axis=0, tiled=True)  26.7 us
    all_to_all x1, starting transfers between devices, on_device(): lax.all_to_all(outgoing, 'page', split_axis=1, concat_axis=1, tiled=True)  22.8 us
    ppermute x1, waiting for transfers between devices, gather_col(): other = lax.ppermute(values, 'col', [(0, 1), (1, 0)])  22 us
    dot_general x1, matrix products, hidden_of(): gate_up = jnp.dot(rows, gateup_full, preferred_element_type=f32)  18.1 us
    dot_general x2, matrix products, down_terms(): lax.dot_general(hidden, weights, contract_last, preferred_element_type=f32)  13.5 us
    ppermute x1, waiting for transfers between devices, on_device(): attn_other = lax.ppermute(attn_terms, 'col', [(0, 1), (1, 0)])  9.08 us
    ppermute x1, waiting for transfers between devices, on_device(): arrived = lax.ppermute(theirs, 'col', [(0, 1), (1, 0)])  8.45 us
  transfers between devices with their start and end apart: 9, of which 8 were waited for; matrix products, arithmetic and copies ran while one was open for 16% of the time, Pallas kernels for 0%

profile of v3, /device:TPU:17, one launch (start us, length us, event | category | flops | bytes accessed | tf_op | source)
XLA Modules:
  0.0 269.7 jit_solution(7650388310026685880)
XLA Ops:
  7.2 2.0 convert.43
  9.3 0.2 copy.45
  9.6 1.4 pad_maximum_fusion.2
  11.4 1.4 collective-permute-start.1
  12.7 7.3 %collective-permute-done.1 = bf16[1,128,1280]{2,1,0:T(8,128)(2,1)S(1)} collective-permute-done((bf16[1,128,1280]{2,1,0:T(8,128)(2,1)S(1)}, bf16[1,128,1280]{2,1,0:T(8,128)(2,1)S(1)}, u32[]{:S(2)}, u32[]{:S(2)}) %collective-permute-start.1) | collective-permute-done | bytes 327712 | tf_op jit(solution)/shard_map/ppermute | solution.py:65
  20.2 0.3 collective-permute-start.2
  20.5 34.9 %collective-permute-done.2 = bf16[2,128,1280]{2,1,0:T(8,128)(2,1)S(1)} collective-permute-done((bf16[2,128,1280]{2,1,0:T(8,128)(2,1)S(1)}, bf16[2,128,1280]{2,1,0:T(8,128)(2,1)S(1)}, u32[]{:S(2)}, u32[]{:S(2)}) %collective-permute-start.2) | collective-permute-done | bytes 655392 | tf_op jit(solution)/shard_map/ppermute | solution.py:65
  55.5 0.8 copy-done.5
  56.5 1.0 collective-permute-start.3
  57.5 27.7 %collective-permute-done.3 = bf16[1,4,128,1280]{3,2,1,0:T(8,128)(2,1)} collective-permute-done((bf16[1,4,128,1280]{3,2,1,0:T(8,128)(2,1)S(1)}, bf16[1,4,128,1280]{3,2,1,0:T(8,128)(2,1)}, u32[]{:S(2)}, u32[]{:S(2)}) %collective-permute-start.3) | collective-permute-done | bytes 1310752 | tf_op jit(solution)/shard_map/ppermute | solution.py:65
  85.2 1.7 select_bitcast_fusion.3
  86.9 1.7 maximum_bitcast_fusion
  88.6 2.7 collective-permute-start.4
  91.3 1.0 collective-permute-start
  92.3 0.2 convert_reduce_fusion
  92.6 0.6 iota_reduce_fusion.1
  94.0 0.3 fusion.40
  94.4 22.0 %collective-permute-done = bf16[1,512,1024]{2,1,0:T(8,128)(2,1)} collective-permute-done((bf16[1,512,1024]{2,1,0:T(8,128)(2,1)}, bf16[1,512,1024]{2,1,0:T(8,128)(2,1)}, u32[]{:S(2)}, u32[]{:S(2)}) %collective-permute-start) | collective-permute-done | bytes 1048608 | tf_op jit(solution)/shard_map/ppermute | solution.py:50
  116.4 1.7 broadcast_select_fusion.1
  118.1 0.5 fusion.8
  118.6 2.3 select_bitcast_fusion.1
  121.0 0.5 pad_maximum_fusion
  121.7 1.9 fusion.31
  123.5 0.2 copy-done.6
  123.9 0.4 copy.41
  125.1 2.1 fusion.2
  127.1 2.3 fusion.35
  129.4 4.3 %fusion.16 = bf16[1,512,2048]{2,1,0:T(8,128)(2,1)} fusion(bf16[512,512]{0,1:T(8,128)(2,1)S(1)} %bitcast.117, bf16[2048,1280]{1,0:T(8,128)(2,1)} %bitcast.110), kind=kOutput, calls=%fused_computation.28 | convolution fusion | flops 1074790400 | bytes 4718592 | tf_op jit(solution)/shard_map/dot_general | solution.py:166
  133.7 1.0 collective-permute-start.5
  134.8 0.7 iota_reduce_fusion
  135.8 0.6 gather_fusion
  136.4 0.8 select_bitcast_fusion.5
  137.2 22.8 %all-to-all-start = ((bf16[2,4,128,128]{3,2,0,1:T(8,128)(2,1)}), bf16[2,4,128,128]{3,2,0,1:T(8,128)(2,1)S(1)}, u32[]{:S(2)}, u32[]{:S(2)}) async-start(bf16[2,4,128,128]{3,2,0,1:T(8,128)(2,1)} %select_bitcast_fusion.5), calls=%async_computation | async-start | bytes 524288 | tf_op jit(solution)/shard_map/all_to_all | solution.py:209
  160.1 6.7 %all-to-all-done = bf16[2,4,128,128]{3,2,0,1:T(8,128)(2,1)S(1)} async-done(((bf16[2,4,128,128]{3,2,0,1:T(8,128)(2,1)}), bf16[2,4,128,128]{3,2,0,1:T(8,128)(2,1)S(1)}, u32[]{:S(2)}, u32[]{:S(2)}) %all-to-all-start) | async-done | bytes 262176 | tf_op jit(solution)/shard_map/all_to_all | solution.py:209
  166.8 0.6 gather_fusion.1
  167.6 3.6 %concatenate.81 = bf16[2,4,128,512]{3,2,0,1:T(8,128)(2,1)} concatenate(bf16[2,4,128,64]{3,2,0,1:T(8,128)(2,1)S(1)} %get-tuple-element.34, bf16[2,4,128,64]{3,2,0,1:T(8,128)(2,1)S(1)} %get-tuple-element.34, bf16[2,4,128,64]{3,2,0,1:T(8,128)(2,1)S(1)} %get-tuple-element.34, bf16[2,4,128,128]{3,2,0,1:T(8,128)(2,1)S(1)} %select_bitcast_fusion.4, ...), dimensions={3} | concatenate | bytes 2097152 | tf_op jit(solution)/shard_map/concatenate | solution.py:220
  171.2 9.1 %collective-permute-done.5 = bf16[1,512,2048]{2,1,0:T(8,128)(2,1)} collective-permute-done((bf16[1,512,2048]{2,1,0:T(8,128)(2,1)}, bf16[1,512,2048]{2,1,0:T(8,128)(2,1)}, u32[]{:S(2)}, u32[]{:S(2)}) %collective-permute-start.5) | collective-permute-done | bytes 2097184 | tf_op jit(solution)/shard_map/ppermute | solution.py:171
  180.3 3.9 %fusion.10 = (f32[512]{0:T(512)S(1)}, bf16[1,512,2048]{2,1,0:T(8,128)(2,1)S(1)}) fusion(bf16[1,512,2048]{2,1,0:T(8,128)(2,1)} %collective-permute-done.5, bf16[1,512,2048]{2,1,0:T(8,128)(2,1)} %fusion.16, bf16[1,512,1024]{2,1,0:T(8,128)(2,1)} %copy-done.4, bf16[1,512,1024]{2,1,0:T(8,128)(2,1)S(1)} %copy-done.3), kind=kLoop, calls=%fused_computation.20 | loop fusion | flops 12582400 | bytes 8390656 | tf_op jit(solution)/shard_map/reduce_sum | solution.py:11
  184.2 1.9 fusion.17
  186.1 26.7 %all-gather.2.cloned.1.call-done = bf16[2048,7680]{1,0:T(8,128)(2,1)} async-done(((bf16[128,7680]{1,0:T(8,128)(2,1)}), bf16[2048,7680]{1,0:T(8,128)(2,1)}) %all-gather.2.cloned.1.call-update) | async-done | bytes 31457296 | tf_op jit(solution)/shard_map/all_gather | solution.py:59
  212.8 18.1 %fusion = f32[512,5120]{1,0:T(8,128)} fusion(bf16[512,2048]{1,0:T(8,128)(2,1)} %fusion.17, bf16[2048,7680]{1,0:T(8,128)(2,1)} %all-gather.2.cloned.1.call-done), kind=kOutput, calls=%fused_computation.2 | convolution fusion | flops 10737418240 | bytes 33554432 | tf_op jit(solution)/shard_map/dot_general | solution.py:235
  230.9 4.8 %fusion.3 = bf16[512,2560]{1,0:T(8,128)(2,1)S(1)} fusion(f32[512,5120]{1,0:T(8,128)} %fusion), kind=kLoop, calls=%fused_computation.12 | loop fusion | flops 7864320 | bytes 13107200 | tf_op jit(solution)/shard_map/convert_element_type | solution.py:236
  235.7 7.3 %fusion.28 = bf16[512,1024]{1,0:T(8,128)(2,1)} fusion(bf16[512,2560]{1,0:T(8,128)(2,1)S(1)} %fusion.3, bf16[2048,7680]{1,0:T(8,128)(2,1)} %all-gather.2.cloned.1.call-done, s32[]{:T(128)S(6)} %select_n.150), kind=kOutput, calls=%fused_computation.44 | convolution fusion | flops 2684878848 | bytes 8912900 | tf_op jit(solution)/shard_map/dot_general | solution.py:239
  243.1 1.2 collective-permute-start.6
  244.3 1.1 copy.46
  245.4 6.2 %fusion.25 = bf16[512,1024]{1,0:T(8,128)(2,1)S(1)} fusion(bf16[512,2560]{1,0:T(8,128)(2,1)} %copy-done.8, bf16[2048,7680]{1,0:T(8,128)(2,1)} %all-gather.2.cloned.1.call-done, s32[]{:T(128)S(6)} %select_n.144), kind=kOutput, calls=%fused_computation.43 | convolution fusion | flops 2684878848 | bytes 8912900 | tf_op jit(solution)/shard_map/dot_general | solution.py:239
  251.6 8.5 %collective-permute-done.6 = bf16[512,1024]{1,0:T(8,128)(2,1)} collective-permute-done((bf16[512,1024]{1,0:T(8,128)(2,1)}, bf16[512,1024]{1,0:T(8,128)(2,1)}, u32[]{:S(2)}, u32[]{:S(2)}) %collective-permute-start.6) | collective-permute-done | bytes 1048608 | tf_op jit(solution)/shard_map/ppermute | solution.py:249
  260.0 2.8 %fusion.22 = bf16[1,512,1024]{2,1,0:T(8,128)(2,1)} fusion(bf16[512,1024]{1,0:T(8,128)(2,1)} %collective-permute-done.6, bf16[512,1024]{1,0:T(8,128)(2,1)S(1)} %fusion.25, bf16[1,512,2048]{2,1,0:T(8,128)(2,1)S(1)} %get-tuple-element.18, s32[]{:T(128)S(6)} %select_n.144), kind=kLoop, calls=%fused_computation.39 | loop fusion | flops 3145728 | bytes 4194308 | tf_op jit(solution)/shard_map/convert_element_type | solution.py:262
  (79 shorter events, 2.8 us)
Async XLA Ops:
  7.2 4.0 %copy-start = (f32[2,128,256]{2,1,0:T(8,128)S(1)}, f32[2,128,256]{2,1,0:T(8,128)}, u32[]{:S(2)}) copy-start(f32[2,128,256]{2,1,0:T(8,128)} %param.18) | copy-start | bytes 786436
  7.2 2.1 copy-start.9
  7.2 205.6 %all-gather.2.cloned.1.call-start = ((), (), s32[]{:S(2)}) async-start(), calls=%async_computation.1 | async-start | bytes 33423360 | tf_op jit(solution)/shard_map/all_gather | solution.py:59
  9.6 1.5 copy-start.10
  9.6 1.7 copy-start.11
  11.4 8.6 %collective-permute-start.1 = (bf16[1,128,1280]{2,1,0:T(8,128)(2,1)S(1)}, bf16[1,128,1280]{2,1,0:T(8,128)(2,1)S(1)}, u32[]{:S(2)}, u32[]{:S(2)}) collective-permute-start(bf16[1,128,1280]{2,1,0:T(8,128)(2,1)S(1)} %pad_maximum_fusion.5), channel_id=1, source_target_pairs={{0,1},{1,0},{2,3},{3,2},{4,5},{5,4},{6,7},{7,6},{8,9},{9,8},{10,11... | collective-permute-start | bytes 983048 | tf_op jit(solution)/shard_map/ppermute | solution.py:65
  20.2 35.2 %collective-permute-start.2 = (bf16[2,128,1280]{2,1,0:T(8,128)(2,1)S(1)}, bf16[2,128,1280]{2,1,0:T(8,128)(2,1)S(1)}, u32[]{:S(2)}, u32[]{:S(2)}) collective-permute-start(bf16[2,128,1280]{2,1,0:T(8,128)(2,1)S(1)} %pad_maximum_fusion.3), channel_id=1, source_target_pairs={{0,2},{1,3},{2,0},{3,1},{4,6},{5,7},{6,4},{7,5},{8,10},{9,11},{10,... | collective-permute-start | bytes 1966088 | tf_op jit(solution)/shard_map/ppermute | solution.py:65
  55.5 0.8 copy-start.5
  56.5 28.7 %collective-permute-start.3 = (bf16[1,4,128,1280]{3,2,1,0:T(8,128)(2,1)S(1)}, bf16[1,4,128,1280]{3,2,1,0:T(8,128)(2,1)}, u32[]{:S(2)}, u32[]{:S(2)}) collective-permute-start(bf16[1,4,128,1280]{3,2,1,0:T(8,128)(2,1)S(1)} %maximum_bitcast_fusion.1), channel_id=1, source_target_pairs={{0,16},{8,24},{16,0},{24,8},{1,17},{9,25},{17,1},{25,9},{2,18},{10... | collective-permute-start | bytes 3932168 | tf_op jit(solution)/shard_map/ppermute | solution.py:65
  86.9 5.4 %copy-start.13 = (s32[4,4]{1,0:T(4,128)S(1)}, s32[4,4]{1,0:T(4,128)}, u32[]{:S(2)}) copy-start(s32[4,4]{1,0:T(4,128)} %param.16) | copy-start | bytes 196
  86.9 7.0 %copy-start.14 = (f32[64]{0:T(128)S(1)}, f32[64]{0:T(128)}, u32[]{:S(2)}) copy-start(f32[64]{0:T(128)} %param.24) | copy-start | bytes 772
  86.9 7.0 %copy-start.16 = (f32[64]{0:T(128)S(1)}, f32[64]{0:T(128)}, u32[]{:S(2)}) copy-start(f32[64]{0:T(128)} %param.25) | copy-start | bytes 772
  88.6 30.0 %collective-permute-start.4 = (bf16[2,4,128,1280]{3,2,1,0:T(8,128)(2,1)}, bf16[2,4,128,1280]{3,2,1,0:T(8,128)(2,1)}, u32[]{:S(2)}, u32[]{:S(2)}) collective-permute-start(bf16[2,4,128,1280]{3,2,1,0:T(8,128)(2,1)} %maximum_bitcast_fusion), channel_id=1, source_target_pairs={{0,8},{8,0},{16,24},{24,16},{1,9},{9,1},{17,25},{25,17},{2,10},{10... | collective-permute-start | bytes 7864328 | tf_op jit(solution)/shard_map/ppermute | solution.py:65
  91.3 25.1 %collective-permute-start = (bf16[1,512,1024]{2,1,0:T(8,128)(2,1)}, bf16[1,512,1024]{2,1,0:T(8,128)(2,1)}, u32[]{:S(2)}, u32[]{:S(2)}) collective-permute-start(bf16[1,512,1024]{2,1,0:T(8,128)(2,1)} %param.14), channel_id=1, source_target_pairs={{0,4},{4,0},{1,5},{5,1},{2,6},{6,2},{3,7},{7,3},{8,12},{12,8},{9,1... | collective-permute-start | bytes 3145736 | tf_op jit(solution)/shard_map/ppermute | solution.py:50
  118.1 3.4 %copy-start.2 = (bf16[1,512,1024]{2,1,0:T(8,128)(2,1)}, bf16[1,512,1024]{2,1,0:T(8,128)(2,1)S(1)}, u32[]{:S(2)}) copy-start(bf16[1,512,1024]{2,1,0:T(8,128)(2,1)S(1)} %get-tuple-element.23) | copy-start | bytes 3145732
  118.1 3.4 %copy-start.4 = (bf16[1,512,1024]{2,1,0:T(8,128)(2,1)}, bf16[1,512,1024]{2,1,0:T(8,128)(2,1)S(1)}, u32[]{:S(2)}) copy-start(bf16[1,512,1024]{2,1,0:T(8,128)(2,1)S(1)} %get-tuple-element.24) | copy-start | bytes 3145732
  121.0 0.7 copy-start.15
  121.5 2.3 copy-start.6
  133.7 46.7 %collective-permute-start.5 = (bf16[1,512,2048]{2,1,0:T(8,128)(2,1)}, bf16[1,512,2048]{2,1,0:T(8,128)(2,1)}, u32[]{:S(2)}, u32[]{:S(2)}) collective-permute-start(bf16[1,512,2048]{2,1,0:T(8,128)(2,1)} %fusion.16), channel_id=1, source_target_pairs={{0,4},{4,0},{1,5},{5,1},{2,6},{6,2},{3,7},{7,3},{8,12},{12,8},{9,1... | collective-permute-start | bytes 6291464 | tf_op jit(solution)/shard_map/ppermute | solution.py:171
  137.2 29.5 %all-to-all-start = ((bf16[2,4,128,128]{3,2,0,1:T(8,128)(2,1)}), bf16[2,4,128,128]{3,2,0,1:T(8,128)(2,1)S(1)}, u32[]{:S(2)}, u32[]{:S(2)}) async-start(bf16[2,4,128,128]{3,2,0,1:T(8,128)(2,1)} %select_bitcast_fusion.5), calls=%async_computation | async-start | bytes 524288 | tf_op jit(solution)/shard_map/all_to_all | solution.py:209
  166.8 13.6 %copy-start.3 = (bf16[1,512,1024]{2,1,0:T(8,128)(2,1)S(1)}, bf16[1,512,1024]{2,1,0:T(8,128)(2,1)}, u32[]{:S(2)}) copy-start(bf16[1,512,1024]{2,1,0:T(8,128)(2,1)} %copy-done.2) | copy-start | bytes 3145732
  171.2 13.0 %copy-start.12 = (f32[2048]{0:T(1024)S(1)}, f32[2048]{0:T(1024)}, u32[]{:S(2)}) copy-start(f32[2048]{0:T(1024)} %param.23) | copy-start | bytes 24580
  235.7 7.4 %copy-start.8 = (bf16[512,2560]{1,0:T(8,128)(2,1)}, bf16[512,2560]{1,0:T(8,128)(2,1)S(1)}, u32[]{:S(2)}) copy-start(bf16[512,2560]{1,0:T(8,128)(2,1)S(1)} %fusion.3) | copy-start | bytes 7864324
  235.7 8.5 %copy-start.7 = (bf16[2,4,128,512]{3,2,0,1:T(8,128)(2,1)S(1)}, bf16[2,4,128,512]{3,2,0,1:T(8,128)(2,1)}, u32[]{:S(2)}) copy-start(bf16[2,4,128,512]{3,2,0,1:T(8,128)(2,1)} %concatenate.81) | copy-start | bytes 3145732
  243.1 16.9 %collective-permute-start.6 = (bf16[512,1024]{1,0:T(8,128)(2,1)}, bf16[512,1024]{1,0:T(8,128)(2,1)}, u32[]{:S(2)}, u32[]{:S(2)}) collective-permute-start(bf16[512,1024]{1,0:T(8,128)(2,1)} %fusion.28), channel_id=1, source_target_pairs={{0,4},{4,0},{1,5},{5,1},{2,6},{6,2},{3,7},{7,3},{8,12},{12,8},{9,1... | collective-permute-start | bytes 3145736 | tf_op jit(solution)/shard_map/ppermute | solution.py:249
  245.4 17.5 %copy-start.1 = (f32[2,128,256]{2,1,0:T(8,128)S(1)}, f32[2,128,256]{2,1,0:T(8,128)}, u32[]{:S(2)}) copy-start(f32[2,128,256]{2,1,0:T(8,128)} %param.18) | copy-start | bytes 786436
Sparse Core Ops, SparseCore 0:
  11.2 201.6 all-gather.1

commit v4 on v3

--- a/solution.py
+++ b/solution.py
@@ -65,11 +65,11 @@
     return lax.ppermute(values, axis, [(i, i ^ bit) for i in range(count)])
 
 
-def gather_doubling(piece):
+def gather_doubling(piece, gathered):
     row_count = lax.axis_size("row")
     page_count = lax.axis_size("page")
     if row_count & (row_count - 1) or page_count & (page_count - 1):
-        return gather_rows(piece)
+        return gather_rows(piece), gathered
     held = piece[None]
     bit = 1
     while bit < page_count:
@@ -79,6 +79,7 @@
             [jnp.where(upper, other, held), jnp.where(upper, held, other)], axis=0
         )
         bit *= 2
+    held, gathered = lax.optimization_barrier((held, gathered))
     held = held[None]
     bit = row_count // 2
     while bit >= 1:
@@ -88,7 +89,7 @@
             [jnp.where(upper, other, held), jnp.where(upper, held, other)], axis=1
         ).reshape(2 * held.shape[0], *held.shape[1:])
         bit //= 2
-    return held.reshape(-1, piece.shape[1])
+    return held.reshape(-1, piece.shape[1]), gathered
 
 
 def on_device(
@@ -130,7 +131,7 @@
     ).astype(bf16)
     ffn_piece = jnp.concatenate([w_gateup[0], w_gateup[1], w_down.T], axis=1).astype(bf16)
     ffn_full = gather_rows(ffn_piece)
-    attn_full = gather_doubling(attn_piece)
+    attn_full, gathered = gather_doubling(attn_piece, gathered)
     gateup_full = ffn_full[:, : 2 * unit_count]
     qkv_width = local_width + 2 * kv_width
     out_t = attn_full[:, qkv_width:]
@@ -241,13 +242,18 @@
         ).astype(bf16)
 
     if col_count == 2:
-        down_at = lambda col: lax.dynamic_slice(
-            ffn_full, (col * local_feat, 2 * unit_count), (local_feat, unit_count)
-        )
+        def down_at(first, width):
+            return lax.dynamic_slice(ffn_full, (first, 2 * unit_count), (width, unit_count))
+
         hidden = hidden_of(ffn_in)
-        theirs = down_terms(hidden, down_at(1 - col_index))
-        arrived = lax.ppermute(theirs, "col", [(0, 1), (1, 0)])
-        mine = lax.optimization_barrier(down_terms(hidden, down_at(col_index)))
+        half = local_feat // 2
+        other_first = (1 - col_index) * local_feat
+        arrivals = []
+        for first in (other_first, other_first + half):
+            theirs = down_terms(hidden, down_at(first, half))
+            arrivals.append(lax.ppermute(theirs, "col", [(0, 1), (1, 0)]))
+        arrived = jnp.concatenate(arrivals, axis=1)
+        mine = lax.optimization_barrier(down_terms(hidden, down_at(col_index * local_feat, local_feat)))
         ffn_sum = (mine.astype(f32) + arrived.astype(f32)).reshape(
             prompt_count, seq_len, local_feat
         )

time: 273 us -> 259 us (0.949)
  waiting for transfers between devices: 143 us -> 132 us
  matrix products: 42 us -> 37.3 us
  local copies, waits for them, and re-layouts: 8.7 us -> 13.4 us
    ppermute x1, waiting for transfers between devices: 22 us -> 0.01 us  [gather_col(): other = lax.ppermute(values, 'col', [(0, 1), (1, 0)])]
    all_gather x1, waiting for transfers between devices: 26.7 us -> 41.1 us  [gather_rows(): full = lax.all_gather(piece, ('row', 'page'), axis=0, tiled=True)]
    dot_general x1, matrix products: 18.1 us -> 14.7 us  [hidden_of(): gate_up = jnp.dot(rows, gateup_full, preferred_element_type=f32)]
    convert_element_type x1, other arithmetic: 4.83 us -> 1.64 us  [hidden_of(): (jax.nn.silu(gate_up[:, :unit_count]) * gate_up[:, unit_count:]).astype(b...]
    ppermute x1 -> x2, waiting for transfers between devices: 8.45 us -> 6.22 us  [on_device(): arrivals.append(lax.ppermute(theirs, 'col', [(0, 1), (1, 0)]))]
    dot_general x2 -> x3, matrix products: 13.5 us -> 12.1 us  [down_terms(): lax.dot_general(hidden, weights, contract_last, preferred_element_type=f32)]
  transfers between devices with their start and end apart: 9 -> 10, of which waited for: 8 -> 9; matrix products, arithmetic and copies ran while one was open for 16% -> 20% of each run, Pallas kernels for 0% -> 0%
where the time goes in v4:
time: 259 us; the launch traced here: 258 us
  waiting for transfers between devices  132 us (51%)
  matrix products  37.3 us (14%)
  starting transfers between devices  32.1 us (12%)
  other arithmetic  27.4 us (11%)
  between operations  15.3 us (6%)
  local copies, waits for them, and re-layouts  13.4 us (5%)
    ppermute x4, waiting for transfers between devices, exchange(): return lax.ppermute(values, axis, [(i, i ^ bit) for i in range(count)])  69.2 us
    all_gather x1, waiting for transfers between devices, gather_rows(): full = lax.all_gather(piece, ('row', 'page'), axis=0, tiled=True)  41.1 us
    all_to_all x1, starting transfers between devices, on_device(): lax.all_to_all(outgoing, 'page', split_axis=1, concat_axis=1, tiled=True)  23 us
    dot_general x1, matrix products, hidden_of(): gate_up = jnp.dot(rows, gateup_full, preferred_element_type=f32)  14.7 us
    dot_general x3, matrix products, down_terms(): lax.dot_general(hidden, weights, contract_last, preferred_element_type=f32)  12.1 us
    ppermute x1, waiting for transfers between devices, on_device(): attn_other = lax.ppermute(attn_terms, 'col', [(0, 1), (1, 0)])  8.33 us
    all_to_all x1, waiting for transfers between devices, on_device(): lax.all_to_all(outgoing, 'page', split_axis=1, concat_axis=1, tiled=True)  7.23 us
    ppermute x2, waiting for transfers between devices, on_device(): arrivals.append(lax.ppermute(theirs, 'col', [(0, 1), (1, 0)]))  6.22 us
  transfers between devices with their start and end apart: 10, of which 9 were waited for; matrix products, arithmetic and copies ran while one was open for 20% of the time, Pallas kernels for 0%

profile of v4, /device:TPU:17, one launch (start us, length us, event | category | flops | bytes accessed | tf_op | source)
XLA Modules:
  0.0 257.6 jit_solution(10446248117116338449)
XLA Ops:
  7.2 2.0 convert.43
  9.6 1.4 pad_maximum_fusion.2
  11.4 1.4 collective-permute-start
  12.7 7.3 %collective-permute-done = bf16[1,128,1280]{2,1,0:T(8,128)(2,1)S(1)} collective-permute-done((bf16[1,128,1280]{2,1,0:T(8,128)(2,1)S(1)}, bf16[1,128,1280]{2,1,0:T(8,128)(2,1)S(1)}, u32[]{:S(2)}, u32[]{:S(2)}) %collective-permute-start) | collective-permute-done | bytes 327712 | tf_op jit(solution)/shard_map/ppermute | solution.py:65
  20.5 1.1 collective-permute-start.2
  21.6 33.9 %collective-permute-done.1 = bf16[2,128,1280]{2,1,0:T(8,128)(2,1)S(1)} collective-permute-done((bf16[2,128,1280]{2,1,0:T(8,128)(2,1)S(1)}, bf16[2,128,1280]{2,1,0:T(8,128)(2,1)S(1)}, u32[]{:S(2)}, u32[]{:S(2)}) %collective-permute-start.1) | collective-permute-done | bytes 655392 | tf_op jit(solution)/shard_map/ppermute | solution.py:65
  55.7 2.2 broadcast_select_fusion.1
  58.0 1.0 collective-permute-start.3
  59.0 27.7 %collective-permute-done.3 = bf16[1,4,128,1280]{3,2,1,0:T(8,128)(2,1)} collective-permute-done((bf16[1,4,128,1280]{3,2,1,0:T(8,128)(2,1)S(1)}, bf16[1,4,128,1280]{3,2,1,0:T(8,128)(2,1)}, u32[]{:S(2)}, u32[]{:S(2)}) %collective-permute-start.3) | collective-permute-done | bytes 1310752 | tf_op jit(solution)/shard_map/ppermute | solution.py:65
  86.7 1.9 select_bitcast_fusion.3
  88.7 1.9 maximum_bitcast_fusion
  90.6 2.6 %collective-permute-start.4 = (bf16[2,4,128,1280]{3,2,1,0:T(8,128)(2,1)}, bf16[2,4,128,1280]{3,2,1,0:T(8,128)(2,1)}, u32[]{:S(2)}, u32[]{:S(2)}) collective-permute-start(bf16[2,4,128,1280]{3,2,1,0:T(8,128)(2,1)} %maximum_bitcast_fusion), channel_id=1, source_target_pairs={{0,8},{8,0},{16,24},{24,16},{1,9},{9,1},{17,25},{25,17},{2,10},{10... | collective-permute-start | bytes 7864328 | tf_op jit(solution)/shard_map/ppermute | solution.py:65
  94.2 0.6 iota_reduce_fusion.1
  94.9 0.6 pad_clamp_fusion.1
  95.5 1.0 fusion.48
  96.5 0.8 fusion.44
  98.1 2.1 select_bitcast_fusion.1
  101.0 1.8 fusion.28
  103.1 1.2 slice.88
  104.3 1.8 copy.41
  106.1 0.8 copy.40
  108.2 2.1 fusion.2
  110.3 2.3 fusion.43
  112.6 4.3 %fusion.16 = bf16[1,512,2048]{2,1,0:T(8,128)(2,1)} fusion(bf16[512,512]{0,1:T(8,128)(2,1)S(1)} %bitcast.117, bf16[2048,1280]{1,0:T(8,128)(2,1)} %bitcast.109), kind=kOutput, calls=%fused_computation.28 | convolution fusion | flops 1074790400 | bytes 4718592 | tf_op jit(solution)/shard_map/dot_general | solution.py:167
  116.9 1.1 collective-permute-start.5
  118.2 0.6 iota_reduce_fusion
  119.1 0.7 gather_fusion
  119.9 0.8 select_bitcast_fusion.5
  120.6 23.0 %all-to-all-start = ((bf16[2,4,128,128]{3,2,0,1:T(8,128)(2,1)}), bf16[2,4,128,128]{3,2,0,1:T(8,128)(2,1)S(1)}, u32[]{:S(2)}, u32[]{:S(2)}) async-start(bf16[2,4,128,128]{3,2,0,1:T(8,128)(2,1)} %select_bitcast_fusion.5), calls=%async_computation | async-start | bytes 524288 | tf_op jit(solution)/shard_map/all_to_all | solution.py:210
  143.7 7.2 %all-to-all-done = bf16[2,4,128,128]{3,2,0,1:T(8,128)(2,1)S(1)} async-done(((bf16[2,4,128,128]{3,2,0,1:T(8,128)(2,1)}), bf16[2,4,128,128]{3,2,0,1:T(8,128)(2,1)S(1)}, u32[]{:S(2)}, u32[]{:S(2)}) %all-to-all-start) | async-done | bytes 262176 | tf_op jit(solution)/shard_map/all_to_all | solution.py:210
  150.9 0.6 gather_fusion.1
  151.6 0.9 fusion.60
  152.5 3.1 %concatenate.61 = bf16[2,4,128,512]{3,2,0,1:T(8,128)(2,1)S(1)} concatenate(bf16[2,4,128,64]{3,2,0,1:T(8,128)(2,1)} %get-tuple-element.38, bf16[2,4,128,64]{3,2,0,1:T(8,128)(2,1)} %get-tuple-element.38, bf16[2,4,128,64]{3,2,0,1:T(8,128)(2,1)} %get-tuple-element.38, bf16[2,4,128,128]{3,2,0,1:T(8,128)(2,1)S(1)} %select_bitcast_fusion.4, bf16[2,4,128,64]{3,2,0,1:T(8,128)(2,1)} %get-tuple-element.37, ...), dimensions={3} | concatenate | bytes 2097152 | tf_op jit(solution)/shard_map/concatenate | solution.py:221
  155.6 8.3 %collective-permute-done.5 = bf16[1,512,2048]{2,1,0:T(8,128)(2,1)} collective-permute-done((bf16[1,512,2048]{2,1,0:T(8,128)(2,1)}, bf16[1,512,2048]{2,1,0:T(8,128)(2,1)}, u32[]{:S(2)}, u32[]{:S(2)}) %collective-permute-start.5) | collective-permute-done | bytes 2097184 | tf_op jit(solution)/shard_map/ppermute | solution.py:172
  164.0 3.5 %fusion.6 = (f32[512]{0:T(512)S(1)}, bf16[1,512,2048]{2,1,0:T(8,128)(2,1)S(1)}) fusion(bf16[1,512,2048]{2,1,0:T(8,128)(2,1)} %collective-permute-done.5, bf16[1,512,2048]{2,1,0:T(8,128)(2,1)} %fusion.16, bf16[1,512,2048]{2,1,0:T(8,128)(2,1)S(1)} %pad_maximum_fusion.1), kind=kLoop, calls=%fused_computation.17 | loop fusion | flops 9436672 | bytes 8390656 | tf_op jit(solution)/shard_map/reduce_sum | solution.py:11
  167.5 1.3 copy-done.2
  168.8 1.9 fusion.23
  170.7 1.1 copy.46
  171.8 41.1 %all-gather.2.cloned.1.call-done = bf16[2048,7680]{1,0:T(8,128)(2,1)} async-done(((bf16[128,7680]{1,0:T(8,128)(2,1)}), bf16[2048,7680]{1,0:T(8,128)(2,1)}) %all-gather.2.cloned.1.call-update) | async-done | bytes 31457296 | tf_op jit(solution)/shard_map/all_gather | solution.py:59
  212.8 14.7 %fusion = f32[512,5120]{1,0:T(8,128)S(1)} fusion(bf16[512,2048]{1,0:T(8,128)(2,1)} %fusion.23, bf16[2048,7680]{1,0:T(8,128)(2,1)} %all-gather.2.cloned.1.call-done), kind=kOutput, calls=%fused_computation.2 | convolution fusion | flops 10737418240 | bytes 33554432 | tf_op jit(solution)/shard_map/dot_general | solution.py:236
  227.6 1.6 fusion.3
  229.2 3.3 %fusion.36 = bf16[512,512]{1,0:T(8,128)(2,1)S(1)} fusion(bf16[512,2560]{1,0:T(8,128)(2,1)S(1)} %fusion.3, bf16[2048,7680]{1,0:T(8,128)(2,1)} %all-gather.2.cloned.1.call-done, s32[]{:T(128)S(6)} %select_n.153), kind=kOutput, calls=%fused_computation.52 | convolution fusion | flops 1342439424 | bytes 5767172 | tf_op jit(solution)/shard_map/dot_general | solution.py:240
  232.5 1.3 collective-permute-start.6
  233.8 3.3 %fusion.39 = bf16[512,512]{1,0:T(8,128)(2,1)S(1)} fusion(bf16[512,2560]{1,0:T(8,128)(2,1)S(1)} %fusion.3, bf16[2048,7680]{1,0:T(8,128)(2,1)} %all-gather.2.cloned.1.call-done, s32[]{:T(128)S(6)} %select_n.154), kind=kOutput, calls=%fused_computation.53 | convolution fusion | flops 1342439424 | bytes 5767172 | tf_op jit(solution)/shard_map/dot_general | solution.py:240
  237.4 5.6 %fusion.33 = bf16[512,1024]{1,0:T(8,128)(2,1)S(1)} fusion(bf16[512,2560]{1,0:T(8,128)(2,1)S(1)} %fusion.3, bf16[2048,7680]{1,0:T(8,128)(2,1)} %all-gather.2.cloned.1.call-done, s32[]{:T(128)S(6)} %select_n.147), kind=kOutput, calls=%fused_computation.46 | convolution fusion | flops 2684878848 | bytes 8912900 | tf_op jit(solution)/shard_map/dot_general | solution.py:240
  243.0 0.6 collective-permute-done.6
  243.6 5.6 %collective-permute-done.7 = bf16[512,512]{1,0:T(8,128)(2,1)S(1)} collective-permute-done((bf16[512,512]{1,0:T(8,128)(2,1)S(1)}, bf16[512,512]{1,0:T(8,128)(2,1)S(1)}, u32[]{:S(2)}, u32[]{:S(2)}) %collective-permute-start.7) | collective-permute-done | bytes 524320 | tf_op jit(solution)/shard_map/ppermute | solution.py:254
  249.2 1.5 fusion.25
  (97 shorter events, 5.9 us)
Async XLA Ops:
  7.2 4.0 %copy-start = (f32[2,128,256]{2,1,0:T(8,128)S(1)}, f32[2,128,256]{2,1,0:T(8,128)}, u32[]{:S(2)}) copy-start(f32[2,128,256]{2,1,0:T(8,128)} %param.18) | copy-start | bytes 786436
  7.2 2.1 copy-start.8
  7.2 205.6 %all-gather.2.cloned.1.call-start = ((), (), s32[]{:S(2)}) async-start(), calls=%async_computation.1 | async-start | bytes 33423360 | tf_op jit(solution)/shard_map/all_gather | solution.py:59
  9.6 1.5 copy-start.11
  9.6 1.7 copy-start.12
  11.4 8.6 %collective-permute-start = (bf16[1,128,1280]{2,1,0:T(8,128)(2,1)S(1)}, bf16[1,128,1280]{2,1,0:T(8,128)(2,1)S(1)}, u32[]{:S(2)}, u32[]{:S(2)}) collective-permute-start(bf16[1,128,1280]{2,1,0:T(8,128)(2,1)S(1)} %pad_maximum_fusion.6), channel_id=1, source_target_pairs={{0,1},{1,0},{2,3},{3,2},{4,5},{5,4},{6,7},{7,6},{8,9},{9,8},{10,11... | collective-permute-start | bytes 983048 | tf_op jit(solution)/shard_map/ppermute | solution.py:65
  20.2 35.2 %collective-permute-start.1 = (bf16[2,128,1280]{2,1,0:T(8,128)(2,1)S(1)}, bf16[2,128,1280]{2,1,0:T(8,128)(2,1)S(1)}, u32[]{:S(2)}, u32[]{:S(2)}) collective-permute-start(bf16[2,128,1280]{2,1,0:T(8,128)(2,1)S(1)} %pad_maximum_fusion.4), channel_id=1, source_target_pairs={{0,2},{1,3},{2,0},{3,1},{4,6},{5,7},{6,4},{7,5},{8,10},{9,11},{10,... | collective-permute-start | bytes 1966088 | tf_op jit(solution)/shard_map/ppermute | solution.py:65
  20.5 35.2 %collective-permute-start.2 = (bf16[1,512,1024]{2,1,0:T(8,128)(2,1)}, bf16[1,512,1024]{2,1,0:T(8,128)(2,1)}, u32[]{:S(2)}, u32[]{:S(2)}) collective-permute-start(bf16[1,512,1024]{2,1,0:T(8,128)(2,1)} %param.14), channel_id=1, source_target_pairs={{0,4},{4,0},{1,5},{5,1},{2,6},{6,2},{3,7},{7,3},{8,12},{12,8},{9,1... | collective-permute-start | bytes 3145736 | tf_op jit(solution)/shard_map/ppermute | solution.py:50
  55.6 3.4 %copy-start.7 = (bf16[4,128,1280]{2,1,0:T(8,128)(2,1)}, bf16[4,128,1280]{2,1,0:T(8,128)(2,1)S(1)}, u32[]{:S(2)}) copy-start(bf16[4,128,1280]{2,1,0:T(8,128)(2,1)S(1)} %pad_maximum_fusion.3) | copy-start | bytes 3932164
  58.0 28.7 %collective-permute-start.3 = (bf16[1,4,128,1280]{3,2,1,0:T(8,128)(2,1)S(1)}, bf16[1,4,128,1280]{3,2,1,0:T(8,128)(2,1)}, u32[]{:S(2)}, u32[]{:S(2)}) collective-permute-start(bf16[1,4,128,1280]{3,2,1,0:T(8,128)(2,1)S(1)} %bitcast.110), channel_id=1, source_target_pairs={{0,16},{8,24},{16,0},{24,8},{1,17},{9,25},{17,1},{25,9},{2,18},{10... | collective-permute-start | bytes 3932168 | tf_op jit(solution)/shard_map/ppermute | solution.py:65
  88.7 2.0 copy-start.4
  88.7 5.3 %copy-start.16 = (s32[4,4]{1,0:T(4,128)S(1)}, s32[4,4]{1,0:T(4,128)}, u32[]{:S(2)}) copy-start(s32[4,4]{1,0:T(4,128)} %param.16) | copy-start | bytes 196
  88.7 6.8 %copy-start.19 = (f32[64]{0:T(128)S(1)}, f32[64]{0:T(128)}, u32[]{:S(2)}) copy-start(f32[64]{0:T(128)} %param.24) | copy-start | bytes 772
  88.7 6.8 %copy-start.21 = (f32[64]{0:T(128)S(1)}, f32[64]{0:T(128)}, u32[]{:S(2)}) copy-start(f32[64]{0:T(128)} %param.25) | copy-start | bytes 772
  90.6 7.5 %collective-permute-start.4 = (bf16[2,4,128,1280]{3,2,1,0:T(8,128)(2,1)}, bf16[2,4,128,1280]{3,2,1,0:T(8,128)(2,1)}, u32[]{:S(2)}, u32[]{:S(2)}) collective-permute-start(bf16[2,4,128,1280]{3,2,1,0:T(8,128)(2,1)} %maximum_bitcast_fusion), channel_id=1, source_target_pairs={{0,8},{8,0},{16,24},{24,16},{1,9},{9,1},{17,25},{25,17},{2,10},{10... | collective-permute-start | bytes 7864328 | tf_op jit(solution)/shard_map/ppermute | solution.py:65
  93.9 4.2 %copy-start.5 = (bf16[1,1,4,128,1280]{4,3,2,1,0:T(8,128)(2,1)S(1)}, bf16[1,1,4,128,1280]{4,3,2,1,0:T(8,128)(2,1)}, u32[]{:S(2)}) copy-start(bf16[1,1,4,128,1280]{4,3,2,1,0:T(8,128)(2,1)} %copy-done.4) | copy-start | bytes 3932164
  94.0 6.3 %copy-start.17 = (pred[512]{0:T(512)(128)(4,1)}, pred[512]{0:T(512)(128)(4,1)S(1)}, u32[]{:S(2)}) copy-start(pred[512]{0:T(512)(128)(4,1)S(1)} %iota_compare_fusion.4) | copy-start | bytes 1540
  94.9 5.4 %copy-start.22 = (s32[4]{0:T(128)}, s32[4]{0:T(128)S(1)}, u32[]{:S(2)}) copy-start(s32[4]{0:T(128)S(1)} %get-tuple-element.11) | copy-start | bytes 52
  100.3 0.7 copy-start.20
  100.8 2.3 copy-start.6
  106.9 0.8 copy-start.9
  106.9 0.9 copy-start.10
  107.3 1.0 copy-start.13
  108.2 2.1 copy-start.14
  108.2 2.1 copy-start.18
  112.6 5.6 %copy-start.23 = (s32[4]{0:T(128)S(1)}, s32[4]{0:T(128)}, u32[]{:S(2)}) copy-start(s32[4]{0:T(128)} %copy-done.22) | copy-start | bytes 52
  116.9 47.1 %collective-permute-start.5 = (bf16[1,512,2048]{2,1,0:T(8,128)(2,1)}, bf16[1,512,2048]{2,1,0:T(8,128)(2,1)}, u32[]{:S(2)}, u32[]{:S(2)}) collective-permute-start(bf16[1,512,2048]{2,1,0:T(8,128)(2,1)} %fusion.16), channel_id=1, source_target_pairs={{0,4},{4,0},{1,5},{5,1},{2,6},{6,2},{3,7},{7,3},{8,12},{12,8},{9,1... | collective-permute-start | bytes 6291464 | tf_op jit(solution)/shard_map/ppermute | solution.py:172
  120.6 30.3 %all-to-all-start = ((bf16[2,4,128,128]{3,2,0,1:T(8,128)(2,1)}), bf16[2,4,128,128]{3,2,0,1:T(8,128)(2,1)S(1)}, u32[]{:S(2)}, u32[]{:S(2)}) async-start(bf16[2,4,128,128]{3,2,0,1:T(8,128)(2,1)} %select_bitcast_fusion.5), calls=%async_computation | async-start | bytes 524288 | tf_op jit(solution)/shard_map/all_to_all | solution.py:210
  155.6 13.2 %copy-start.15 = (f32[2048]{0:T(1024)S(1)}, f32[2048]{0:T(1024)}, u32[]{:S(2)}) copy-start(f32[2048]{0:T(1024)} %param.23) | copy-start | bytes 24580
  167.5 1.3 copy-start.2
  232.5 11.1 %collective-permute-start.6 = (bf16[512,512]{1,0:T(8,128)(2,1)S(1)}, bf16[512,512]{1,0:T(8,128)(2,1)S(1)}, u32[]{:S(2)}, u32[]{:S(2)}) collective-permute-start(bf16[512,512]{1,0:T(8,128)(2,1)S(1)} %fusion.36), channel_id=1, source_target_pairs={{0,4},{4,0},{1,5},{5,1},{2,6},{6,2},{3,7},{7,3},{8,12},{12,8},{9,1... | collective-permute-start | bytes 1572872 | tf_op jit(solution)/shard_map/ppermute | solution.py:254
  237.1 12.1 %copy-start.3 = (bf16[1,512,2048]{2,1,0:T(8,128)(2,1)S(1)}, bf16[1,512,2048]{2,1,0:T(8,128)(2,1)}, u32[]{:S(2)}) copy-start(bf16[1,512,2048]{2,1,0:T(8,128)(2,1)} %copy-done.2) | copy-start | bytes 6291460
  237.1 12.1 %collective-permute-start.7 = (bf16[512,512]{1,0:T(8,128)(2,1)S(1)}, bf16[512,512]{1,0:T(8,128)(2,1)S(1)}, u32[]{:S(2)}, u32[]{:S(2)}) collective-permute-start(bf16[512,512]{1,0:T(8,128)(2,1)S(1)} %fusion.39), channel_id=1, source_target_pairs={{0,4},{4,0},{1,5},{5,1},{2,6},{6,2},{3,7},{7,3},{8,12},{12,8},{9,1... | collective-permute-start | bytes 1572872 | tf_op jit(solution)/shard_map/ppermute | solution.py:254
  237.4 13.3 %copy-start.1 = (f32[2,128,256]{2,1,0:T(8,128)S(1)}, f32[2,128,256]{2,1,0:T(8,128)}, u32[]{:S(2)}) copy-start(f32[2,128,256]{2,1,0:T(8,128)} %param.18) | copy-start | bytes 786436
Sparse Core Ops, SparseCore 0:
  11.1 201.6 all-gather.1
